TPU v7x, 128 devices: a whole 4x4x4 slice. The times are simulated.
128 devices in a mesh: clip: 16 (over y, z_lo, core), tile: 8 (over x, z_hi).
Axes of the slice: x: 4, y: 4, z: 4 (z_hi: 2, z_lo: 2; z = z_hi * 2 + z_lo), core: 2. Of those that a mesh axis runs over, the one named last changes fastest.
Arguments:
- features: bfloat16 [16, 3, 8, 128, 512], P('clip', None, 'tile'), may hold values from -80 to 80
- target: bfloat16 [16, 3, 8, 128, 256], P('clip', None, 'tile'), may hold values from -6 to 6
- gn_gain: float32 [512], replicated, may hold values from 0.5 to 1.5
- attn_query: bfloat16 [512, 512], replicated
- attn_key: bfloat16 [512, 512], replicated
- attn_value: bfloat16 [512, 512], replicated, may hold values from -0.25 to 0.25
- attn_out: bfloat16 [512, 512], replicated, may hold values from -0.25 to 0.25
- conv_weight: bfloat16 [3, 3, 3, 512, 256], replicated, may hold values from -0.0546875 to 0.0546875
- conv_bias: float32 [256], replicated, may hold values from -3 to 3
- percept: bfloat16 [256, 256], replicated, may hold values from -0.375 to 0.375
- lpips_weight: float32 [256], replicated, may hold values from 0.2 to 2
- crop_owner: int32 [16, 64, 1], P('clip'), may hold values from 0 to 7; in each aligned block of 8 rows (0 to 7, 8 to 15, ..., all dimensions but the last counted through in order) at most 2 rows name the same one
- crop_frame: int32 [16, 64], P('clip'), may hold values from 0 to 2
- crop_col: int32 [16, 64], P('clip'), may hold values from 0 to 64
Outputs:
- decoded: bfloat16 [16, 3, 8, 128, 256], P('clip', None, 'tile')
- conv_grad: float32 [3, 3, 3, 512, 256], replicated
- distances: float32 [16, 64], P('clip', 'tile')
Inputs may be any that keep to these rules, and one draw needn't show every extreme that they name: `crop_owner`: in each clip the crops form aligned blocks of 8, block b being scored by tile b; in each block no tile owns more than 2 crops, and in some block a tile owns exactly 2.
All inputs are finite; a program needn't handle non-finite values.
Results may differ from a plain program's by a relative error of at most 0.013.
Values may be sent and summed in bfloat16 or wider, within the bound.
A program may use at most 128 MiB of HBM per device.

v0:
```python
import jax
import jax.numpy as jnp
from jax import lax
from jax.sharding import PartitionSpec as P

GROUPS = 32
CROPW = 64
CAP = 2


EPSILON = 1e-06


def padded_2(block, sides, width):
    for axis, dim in sides:
        count = lax.axis_size(axis)
        forward = [(i, i + 1) for i in range(count - 1)]
        backward = [(target, source) for source, target in forward]
        low = lax.ppermute(
            lax.slice_in_dim(block, block.shape[dim] - width, None, axis=dim), axis, forward
        )
        high = lax.ppermute(lax.slice_in_dim(block, 0, width, axis=dim), axis, backward)
        block = jnp.concatenate([low, block, high], axis=dim)
    return block


def normalize(grouped, first, second, total, gain):
    mean = first / total
    spread = second / total - mean * mean
    scaled = (grouped - mean[None, :, None]) * lax.rsqrt(spread + EPSILON)[None, :, None]
    return (scaled.reshape(grouped.shape[0], -1) * gain[None, :]).astype(jnp.bfloat16)


def prepare(field):
    first_frame = field[0:1]
    timed = jnp.concatenate([first_frame, first_frame, field], axis=0)
    return jnp.pad(timed, ((0, 0), (0, 0), (1, 1), (0, 0)))


def conv_forward(padded, conv_weight, frames, rows, cols):
    width = padded.shape[-1]
    total = jnp.zeros((frames * rows * cols, conv_weight.shape[-1]), jnp.float32)
    for offset_t in range(3):
        for offset_y in range(3):
            for offset_x in range(3):
                tap = padded[
                    offset_t : offset_t + frames,
                    offset_y : offset_y + rows,
                    offset_x : offset_x + cols,
                ].reshape(-1, width)
                total = total + jnp.dot(
                    tap,
                    conv_weight[offset_t, offset_y, offset_x],
                    preferred_element_type=jnp.float32,
                )
    return total


def conv_backward(padded, grad_rows, frames, rows, cols):
    width = padded.shape[-1]
    parts = []
    for offset_t in range(3):
        for offset_y in range(3):
            for offset_x in range(3):
                tap = padded[
                    offset_t : offset_t + frames,
                    offset_y : offset_y + rows,
                    offset_x : offset_x + cols,
                ].reshape(-1, width)
                parts.append(
                    lax.dot_general(
                        tap, grad_rows, (((0,), (0,)), ((), ())), preferred_element_type=jnp.float32
                    )
                )
    return jnp.stack(parts).reshape(3, 3, 3, width, grad_rows.shape[-1])


def perceive(crop, table):
    mapped = jax.nn.gelu(jnp.dot(crop, table, precision=lax.Precision.HIGHEST))
    return mapped * lax.rsqrt(jnp.mean(mapped * mapped, axis=-1, keepdims=True) + EPSILON)


def crop_distance(crop, other, percept, lpips_weight):
    table = percept.astype(jnp.float32)
    gap = perceive(crop, table) - perceive(other, table)
    return jnp.mean(jnp.sum(gap * gap * lpips_weight[None, :], axis=-1))


def crop_eval(crop, other, percept, lpips_weight):
    other_wide = other.astype(jnp.float32)
    value, pull = jax.vjp(
        lambda moving: crop_distance(moving, other_wide, percept, lpips_weight),
        crop.astype(jnp.float32),
    )
    return (value, pull(jnp.ones((), jnp.float32))[0])


def on_device(
    features,
    target,
    gn_gain,
    attn_query,
    attn_key,
    attn_value,
    attn_out,
    conv_weight,
    conv_bias,
    percept,
    lpips_weight,
    crop_owner,
    crop_frame,
    crop_col,
):
    tiles = lax.axis_size("tile")
    mine = lax.axis_index("tile")
    frames, rows_dev, cols, width = features.shape[1:]
    outputs = conv_weight.shape[-1]
    cells = rows_dev * CROPW
    zero = jnp.zeros((), jnp.int32)
    inputs = features[0].reshape(-1, width)
    grouped = inputs.astype(jnp.float32).reshape(inputs.shape[0], GROUPS, width // GROUPS)
    first, second = lax.psum(
        (jnp.sum(grouped, axis=(0, 2)), jnp.sum(grouped * grouped, axis=(0, 2))), "tile"
    )
    total = jnp.float32(inputs.shape[0] * tiles * (width // GROUPS))
    normed = normalize(grouped, first, second, total, gn_gain)
    queries = jnp.dot(normed, attn_query, preferred_element_type=jnp.float32).astype(jnp.bfloat16)
    scale = 1.0 / jnp.sqrt(jnp.float32(width))
    count = queries.shape[0]
    keys_local = jnp.dot(normed, attn_key, preferred_element_type=jnp.float32).astype(jnp.bfloat16)
    values_local = jnp.dot(normed, attn_value, preferred_element_type=jnp.float32).astype(
        jnp.bfloat16
    )
    peak = jnp.full((count,), -1e30, jnp.float32)
    scores = (
        lax.dot_general(
            queries,
            lax.all_gather(keys_local, "tile", axis=0, tiled=True),
            (((1,), (1,)), ((), ())),
            preferred_element_type=jnp.float32,
        )
        * scale
    )
    new_peak = jnp.maximum(peak, jnp.max(scores, axis=1))
    weights = jnp.exp(scores - new_peak[:, None])
    totals = jnp.sum(weights, axis=1)
    summed = jnp.dot(
        weights.astype(jnp.bfloat16),
        lax.all_gather(values_local, "tile", axis=0, tiled=True),
        preferred_element_type=jnp.float32,
    )
    mixed = (summed / totals[:, None]).astype(jnp.bfloat16)
    hidden = (
        inputs.astype(jnp.float32) + jnp.dot(mixed, attn_out, preferred_element_type=jnp.float32)
    ).astype(jnp.bfloat16)
    field = hidden.reshape(frames, rows_dev, cols, width)
    rimmed = padded_2(field, (("tile", 1),), 1)
    padded = prepare(rimmed)
    decoded = (
        (conv_forward(padded, conv_weight, frames, rows_dev, cols) + conv_bias[None, :])
        .astype(jnp.bfloat16)
        .reshape(frames, rows_dev, cols, outputs)
    )
    owners = crop_owner[0, :, 0].reshape(tiles, -1)
    per_block = owners.shape[1]
    frame_list = crop_frame[0]
    col_list = crop_col[0]
    tile_ids = jnp.arange(tiles, dtype=jnp.int32)
    slot_ids = jnp.arange(CAP, dtype=jnp.int32)
    owned_hits = (owners[:, :, None] == tile_ids[None, None, :]).astype(jnp.int32)
    ranks = jnp.sum(jnp.cumsum(owned_hits, axis=1) * owned_hits, axis=2) - 1
    own_match = (owners[:, None, :] == mine) & (ranks[:, None, :] == slot_ids[None, :, None])
    crop_ids = jnp.arange(tiles * per_block, dtype=jnp.int32).reshape(tiles, 1, per_block)
    crop_index = jnp.sum(jnp.where(own_match, crop_ids, 0), axis=2).reshape(-1)
    own_valid = jnp.any(own_match, axis=2).reshape(-1)
    slot_frames = frame_list[crop_index]
    slot_cols = col_list[crop_index]

    def cut(source, frame, col):
        start = (frame, zero, col, zero)
        return lax.dynamic_slice(source, start, (1, rows_dev, CROPW, outputs)).reshape(
            cells, outputs
        )

    made = jax.vmap(cut, in_axes=(None, 0, 0))(decoded, slot_frames, slot_cols)
    wanted = jax.vmap(cut, in_axes=(None, 0, 0))(target[0], slot_frames, slot_cols)
    packed = jnp.where(
        own_valid[:, None, None, None],
        jnp.stack((made, wanted), axis=1),
        jnp.zeros((), jnp.bfloat16),
    )
    packed = packed.reshape(tiles, CAP, 2, cells, outputs)
    arrived = lax.all_to_all(packed, "tile", split_axis=0, concat_axis=0, tiled=True)
    my_owners = lax.dynamic_slice_in_dim(owners, mine, 1, 0)[0]
    my_ranks = lax.dynamic_slice_in_dim(ranks, mine, 1, 0)[0]
    eval_match = (my_owners[None, None, :] == tile_ids[:, None, None]) & (
        my_ranks[None, None, :] == slot_ids[None, :, None]
    )
    eval_valid = jnp.any(eval_match, axis=2).reshape(-1)
    flat = arrived.reshape(-1, 2, cells, outputs)
    dists, grads = jax.vmap(lambda crop, other: crop_eval(crop, other, percept, lpips_weight))(
        flat[:, 0], flat[:, 1]
    )
    sending = (
        jnp.where(eval_valid[:, None, None], grads, 0.0)
        .astype(jnp.bfloat16)
        .reshape(tiles, CAP, cells, outputs)
    )
    eval_scores = jnp.where(eval_valid, dists, 0.0).reshape(tiles, CAP)
    distances = jnp.sum(eval_scores[:, :, None] * eval_match.astype(jnp.float32), axis=(0, 1))[
        None, :
    ]
    returned = lax.all_to_all(sending, "tile", split_axis=0, concat_axis=0, tiled=True).reshape(
        -1, cells, outputs
    )

    def add_slot(index, grad_map):
        start = (slot_frames[index], zero, slot_cols[index], zero)
        current = lax.dynamic_slice(grad_map, start, (1, rows_dev, CROPW, outputs))
        update = returned[index].astype(jnp.float32).reshape(1, rows_dev, CROPW, outputs)
        return lax.dynamic_update_slice(grad_map, current + update, start)

    grad_map = lax.fori_loop(
        0, tiles * CAP, add_slot, jnp.zeros((frames, rows_dev, cols, outputs), jnp.float32)
    )
    grad_field = grad_map.astype(jnp.bfloat16)
    local_grad = conv_backward(padded, grad_field.reshape(-1, outputs), frames, rows_dev, cols)
    conv_total = lax.psum(local_grad, ("clip", "tile"))
    return (decoded[None], conv_total, distances)


def solution(mesh):
    return jax.shard_map(
        on_device,
        mesh=mesh,
        in_specs=(
            P("clip", None, "tile", None, None),
            P("clip", None, "tile", None, None),
            P(),
            P(),
            P(),
            P(),
            P(),
            P(),
            P(),
            P(),
            P(),
            P("clip", None, None),
            P("clip", None),
            P("clip", None),
        ),
        out_specs=(P("clip", None, "tile", None, None), P(), P("clip", "tile")),
        check_vma=False,
    )
```

profile of v0, /device:TPU:1, one launch (start us, length us, event | category | flops | bytes accessed | tf_op | source)
XLA Modules:
  0.0 646.4 jit_solution(14951101633224156884)
XLA Ops:
  8.8 22.1 %all-reduce.1 = (f32[32]{0:T(128)S(1)}, f32[32]{0:T(128)S(1)}) all-reduce(f32[32]{0:T(128)S(1)} %reduce_sum.117, f32[32]{0:T(128)S(1)} %reduce_sum.114), channel_id=1, replica_groups=mesh['clip'=16,'tile'=8] {'tile'}, use_global_device_ids=true, to_apply=%region_5.0 | all-reduce | flops 64 | bytes 512 | tf_op jit(solution)/shard_map/psum | solution.py:122
  32.3 2.2 convolution_convert_fusion.1
  34.6 2.2 convolution_convert_fusion
  39.4 58.6 %all-gather.3.cloned.1.call-done = bf16[3072,512]{1,0:T(8,128)(2,1)} async-done(((bf16[384,512]{1,0:T(8,128)(2,1)}), bf16[3072,512]{1,0:T(8,128)(2,1)}) %all-gather.3.cloned.1.call-update) | async-done | bytes 3145744 | tf_op jit(solution)/shard_map/all_gather | solution.py:138
  98.0 5.7 fusion.223
  103.8 3.1 fusion
  106.9 54.9 %all-gather.5.cloned.1.call-done = bf16[3072,512]{1,0:T(8,128)(2,1)} async-done(((bf16[384,512]{1,0:T(8,128)(2,1)}), bf16[3072,512]{1,0:T(8,128)(2,1)}) %all-gather.5.cloned.1.call-update) | async-done | bytes 3145744 | tf_op jit(solution)/shard_map/all_gather | solution.py:149
  161.8 5.1 fusion.6
  168.4 5.5 collective-permute-start
  180.0 7.2 %collective-permute-done = bf16[3,1,128,512]{2,3,0,1:T(8,128)(2,1)S(1)} collective-permute-done((bf16[3,1,128,512]{2,3,0,1:T(8,128)(2,1)S(1)}, bf16[3,1,128,512]{2,3,0,1:T(8,128)(2,1)S(1)}, u32[]{:S(2)}, u32[]{:S(2)}) %collective-permute-start) | collective-permute-done | bytes 393248 | tf_op jit(solution)/shard_map/ppermute | solution.py:19
  188.5 4.0 pad_slice_fusion.1
  199.4 1.9 copy.100
  207.1 2.0 copy.103
  209.1 2.0 copy.105
  211.0 2.0 copy.106
  224.5 1.9 copy.117
  230.3 2.1 fusion.142
  232.4 2.1 fusion.122
  240.2 2.1 fusion.115
  267.4 2.0 convolution_add_fusion.7
  275.6 2.1 convolution_add_fusion.2
  280.4 2.5 gather_fusion.2
  284.1 2.2 maximum_select_fusion
  286.3 5.9 all-to-all-start
  292.6 15.3 %all-to-all-done = bf16[8,2,2,64,256]{4,3,1,2,0:T(8,128)(2,1)} async-done(((bf16[8,2,2,64,256]{4,3,1,2,0:T(8,128)(2,1)}), bf16[8,2,2,64,256]{4,3,1,2,0:T(8,128)(2,1)}, u32[]{:S(2)}, u32[]{:S(2)}) %all-to-all-start) | async-done | bytes 1048608 | tf_op jit(solution)/shard_map/all_to_all | solution.py:193
  311.5 2.6 fusion.5
  314.0 4.1 all-to-all-start.1
  318.2 9.0 %all-to-all-done.1 = bf16[8,2,64,256]{3,2,1,0:T(8,128)(2,1)} async-done(((bf16[8,2,64,256]{3,2,1,0:T(8,128)(2,1)}), bf16[8,2,64,256]{3,2,1,0:T(8,128)(2,1)}, u32[]{:S(2)}, u32[]{:S(2)}) %all-to-all-start.1) | async-done | bytes 524320 | tf_op jit(solution)/shard_map/all_to_all | solution.py:213
  328.0 111.2 %while.13 = (s32[]{:T(128)}, f32[3,1,128,256]{3,2,1,0:T(8,128)}, s32[16]{0:T(128)S(1)}, s32[16]{0:T(128)S(1)}, bf16[16,64,256]{2,1,0:T(8,128)(2,1)}, /*index=5*/s32[]{:T(128)}, s32[]{:T(128)}, s32[]{:T(128)}, s32[]{:T(128)}) while((s32[]{:T(128)}, f32[3,1,128,256]{3,2,1,0:T(8,128)}, s32[16]{0:T(128)S(1)}, s32[16]{0:T(128)S(1)}, ...), condition=%wide.region_17.18_spmd, body=%wide.region_16.17_spmd.sunk | while | flops 32776 | bytes 295121 | solution.py:223
  449.5 5.3 copy-done.4
  455.6 172.4 %all-reduce.4.cloned.1.call-done = f32[3,3,3,512,256]{4,3,2,1,0:T(8,128)} async-done(((f32[3,3,3,512,256]{4,3,2,1,0:T(8,128)}), f32[3,3,3,512,256]{4,3,2,1,0:T(8,128)}) %all-reduce.4.cloned.1.call-update) | async-done | bytes 14155792 | tf_op jit(solution)/shard_map/psum | solution.py:228
  628.0 11.9 %copy.174 = f32[3,3,3,512,256]{4,3,2,1,0:T(8,128)} copy(f32[3,3,3,512,256]{4,3,2,1,0:T(8,128)} %all-reduce.4.cloned.1.call-done) | data formatting | bytes 28311552
  (269 shorter events, 156.0 us)
Async XLA Ops:
  7.2 90.9 %copy-start = (bf16[512,512]{1,0:T(8,128)(2,1)S(1)}, bf16[512,512]{1,0:T(8,128)(2,1)}, u32[]{:S(2)}) copy-start(bf16[512,512]{1,0:T(8,128)(2,1)} %param.19) | copy-start | bytes 1572868
  7.2 90.9 %all-gather.3.cloned.1.call-start = ((), (), s32[]{:S(2)}) async-start(), calls=%async_computation.2 | async-start | bytes 3538944 | tf_op jit(solution)/shard_map/all_gather | solution.py:138
  34.5 127.2 %all-gather.5.cloned.1.call-start = ((), (), s32[]{:S(2)}) async-start(), calls=%async_computation.3 | async-start | bytes 3538944 | tf_op jit(solution)/shard_map/all_gather | solution.py:149
  36.7 125.0 %copy-start.9 = (bf16[1,3,1,128,512]{4,3,2,1,0:T(8,128)(2,1)S(1)}, bf16[1,3,1,128,512]{4,3,2,1,0:T(8,128)(2,1)}, u32[]{:S(2)}) copy-start(bf16[1,3,1,128,512]{4,3,2,1,0:T(8,128)(2,1)} %param.16) | copy-start | bytes 1179652
  36.7 125.0 %copy-start.31 = (bf16[512,512]{1,0:T(8,128)(2,1)S(1)}, bf16[512,512]{1,0:T(8,128)(2,1)}, u32[]{:S(2)}) copy-start(bf16[512,512]{1,0:T(8,128)(2,1)} %param.22) | copy-start | bytes 1572868
  106.9 67.8 %copy-start.2 = (s32[1,64]{1,0:T(1,128)S(1)}, s32[1,64]{1,0:T(1,128)}, u32[]{:S(2)}) copy-start(s32[1,64]{1,0:T(1,128)} %param.29) | copy-start | bytes 772
  161.8 13.6 %copy-start.3 = (s32[1,64]{1,0:T(1,128)S(1)}, s32[1,64]{1,0:T(1,128)}, u32[]{:S(2)}) copy-start(s32[1,64]{1,0:T(1,128)} %param.28) | copy-start | bytes 772
  161.8 14.3 %copy-start.25 = (bf16[1,3,1,128,256]{4,3,2,1,0:T(8,128)(2,1)S(1)}, bf16[1,3,1,128,256]{4,3,2,1,0:T(8,128)(2,1)}, u32[]{:S(2)}) copy-start(bf16[1,3,1,128,256]{4,3,2,1,0:T(8,128)(2,1)} %param.17) | copy-start | bytes 589828
  167.1 12.9 %collective-permute-start.1 = (bf16[3,1,128,512]{2,3,0,1:T(8,128)(2,1)S(1)}, bf16[3,1,128,512]{2,3,0,1:T(8,128)(2,1)S(1)}, u32[]{:S(2)}, u32[]{:S(2)}) collective-permute-start(bf16[3,1,128,512]{2,3,0,1:T(8,128)(2,1)S(1)} %copy.97), channel_id=1, source_target_pairs={{1,0},{2,1},{3,2},{4,3},{5,4},{6,5},{7,6},{9,8},{10,9},{11,10},{12... | collective-permute-start | bytes 1179656 | tf_op jit(solution)/shard_map/ppermute | solution.py:22
  168.4 18.9 %collective-permute-start = (bf16[3,1,128,512]{2,3,0,1:T(8,128)(2,1)S(1)}, bf16[3,1,128,512]{2,3,0,1:T(8,128)(2,1)S(1)}, u32[]{:S(2)}, u32[]{:S(2)}) collective-permute-start(bf16[3,1,128,512]{2,3,0,1:T(8,128)(2,1)S(1)} %copy.97), channel_id=1, source_target_pairs={{0,1},{1,2},{2,3},{3,4},{4,5},{5,6},{6,7},{8,9},{9,10},{10,11},{11... | collective-permute-start | bytes 1179656 | tf_op jit(solution)/shard_map/ppermute | solution.py:19
  211.0 33.2 %copy-start.8 = (bf16[3,1,128,512]{2,3,0,1:T(8,128)(2,1)S(1)}, bf16[3,1,128,512]{2,3,0,1:T(8,128)(2,1)}, u32[]{:S(2)}) copy-start(bf16[3,1,128,512]{2,3,0,1:T(8,128)(2,1)} %get-tuple-element.144) | copy-start | bytes 1179652
  245.2 8.5 %copy-start.23 = (bf16[3,1,128,512]{3,2,0,1:T(8,128)(2,1)S(1)}, bf16[3,1,128,512]{3,2,0,1:T(8,128)(2,1)}, u32[]{:S(2)}) copy-start(bf16[3,1,128,512]{3,2,0,1:T(8,128)(2,1)} %copy.107) | copy-start | bytes 1179652
  245.2 9.8 %copy-start.21 = (bf16[3,1,128,512]{3,2,0,1:T(8,128)(2,1)S(1)}, bf16[3,1,128,512]{3,2,0,1:T(8,128)(2,1)}, u32[]{:S(2)}) copy-start(bf16[3,1,128,512]{3,2,0,1:T(8,128)(2,1)} %copy.108) | copy-start | bytes 1179652
  245.2 11.1 %copy-start.20 = (bf16[3,1,128,512]{3,2,0,1:T(8,128)(2,1)S(1)}, bf16[3,1,128,512]{3,2,0,1:T(8,128)(2,1)}, u32[]{:S(2)}) copy-start(bf16[3,1,128,512]{3,2,0,1:T(8,128)(2,1)} %copy.109) | copy-start | bytes 1179652
  245.2 12.3 %copy-start.13 = (bf16[3,1,128,512]{3,2,0,1:T(8,128)(2,1)S(1)}, bf16[3,1,128,512]{3,2,0,1:T(8,128)(2,1)}, u32[]{:S(2)}) copy-start(bf16[3,1,128,512]{3,2,0,1:T(8,128)(2,1)} %copy.110) | copy-start | bytes 1179652
  245.2 13.6 %copy-start.19 = (bf16[3,1,128,512]{3,2,0,1:T(8,128)(2,1)S(1)}, bf16[3,1,128,512]{3,2,0,1:T(8,128)(2,1)}, u32[]{:S(2)}) copy-start(bf16[3,1,128,512]{3,2,0,1:T(8,128)(2,1)} %copy.111) | copy-start | bytes 1179652
  246.8 13.2 %copy-start.18 = (bf16[3,1,128,512]{3,2,0,1:T(8,128)(2,1)S(1)}, bf16[3,1,128,512]{3,2,0,1:T(8,128)(2,1)}, u32[]{:S(2)}) copy-start(bf16[3,1,128,512]{3,2,0,1:T(8,128)(2,1)} %copy.112) | copy-start | bytes 1179652
  248.2 13.0 %copy-start.12 = (bf16[3,1,128,512]{3,2,0,1:T(8,128)(2,1)S(1)}, bf16[3,1,128,512]{3,2,0,1:T(8,128)(2,1)}, u32[]{:S(2)}) copy-start(bf16[3,1,128,512]{3,2,0,1:T(8,128)(2,1)} %copy.113) | copy-start | bytes 1179652
  249.6 12.9 %copy-start.17 = (bf16[3,1,128,512]{3,2,0,1:T(8,128)(2,1)S(1)}, bf16[3,1,128,512]{3,2,0,1:T(8,128)(2,1)}, u32[]{:S(2)}) copy-start(bf16[3,1,128,512]{3,2,0,1:T(8,128)(2,1)} %copy.114) | copy-start | bytes 1179652
  251.0 12.7 %copy-start.16 = (bf16[3,1,128,512]{3,2,0,1:T(8,128)(2,1)S(1)}, bf16[3,1,128,512]{3,2,0,1:T(8,128)(2,1)}, u32[]{:S(2)}) copy-start(bf16[3,1,128,512]{3,2,0,1:T(8,128)(2,1)} %copy.115) | copy-start | bytes 1179652
  252.4 12.5 %copy-start.11 = (bf16[3,1,128,512]{3,2,0,1:T(8,128)(2,1)S(1)}, bf16[3,1,128,512]{3,2,0,1:T(8,128)(2,1)}, u32[]{:S(2)}) copy-start(bf16[3,1,128,512]{3,2,0,1:T(8,128)(2,1)} %copy.116) | copy-start | bytes 1179652
  253.7 12.5 %copy-start.15 = (bf16[3,1,128,512]{3,2,0,1:T(8,128)(2,1)S(1)}, bf16[3,1,128,512]{3,2,0,1:T(8,128)(2,1)}, u32[]{:S(2)}) copy-start(bf16[3,1,128,512]{3,2,0,1:T(8,128)(2,1)} %copy.117) | copy-start | bytes 1179652
  255.0 12.4 %copy-start.14 = (bf16[3,1,128,512]{3,2,0,1:T(8,128)(2,1)S(1)}, bf16[3,1,128,512]{3,2,0,1:T(8,128)(2,1)}, u32[]{:S(2)}) copy-start(bf16[3,1,128,512]{3,2,0,1:T(8,128)(2,1)} %copy.118) | copy-start | bytes 1179652
  257.5 12.8 %copy-start.10 = (f32[384,256]{1,0:T(8,128)S(1)}, f32[384,256]{1,0:T(8,128)}, u32[]{:S(2)}) copy-start(f32[384,256]{1,0:T(8,128)} %fusion.122) | copy-start | bytes 1179652
  275.6 17.0 %copy-start.26 = (f32[256]{0:T(256)S(1)}, f32[256]{0:T(256)}, u32[]{:S(2)}) copy-start(f32[256]{0:T(256)} %param.26) | copy-start | bytes 3076
  282.9 26.4 %copy-start.32 = (bf16[256,256]{1,0:T(8,128)(2,1)S(1)}, bf16[256,256]{1,0:T(8,128)(2,1)}, u32[]{:S(2)}) copy-start(bf16[256,256]{1,0:T(8,128)(2,1)} %param.25) | copy-start | bytes 393220
  286.3 21.7 %all-to-all-start = ((bf16[8,2,2,64,256]{4,3,1,2,0:T(8,128)(2,1)}), bf16[8,2,2,64,256]{4,3,1,2,0:T(8,128)(2,1)}, u32[]{:S(2)}, u32[]{:S(2)}) async-start(bf16[8,2,2,64,256]{4,3,1,2,0:T(8,128)(2,1)} %maximum_select_fusion), calls=%async_computation | async-start | bytes 2097152 | tf_op jit(solution)/shard_map/all_to_all | solution.py:193
  310.5 17.5 %copy-start.28 = (s32[16]{0:T(128)S(1)}, s32[16]{0:T(128)}, u32[]{:S(2)}) copy-start(s32[16]{0:T(128)} %copy-done.27) | copy-start | bytes 196
  310.5 17.5 %copy-start.30 = (s32[16]{0:T(128)S(1)}, s32[16]{0:T(128)}, u32[]{:S(2)}) copy-start(s32[16]{0:T(128)} %copy-done.29) | copy-start | bytes 196
  314.0 13.2 %all-to-all-start.1 = ((bf16[8,2,64,256]{3,2,1,0:T(8,128)(2,1)}), bf16[8,2,64,256]{3,2,1,0:T(8,128)(2,1)}, u32[]{:S(2)}, u32[]{:S(2)}) async-start(bf16[8,2,64,256]{3,2,1,0:T(8,128)(2,1)} %bitcast.524), calls=%async_computation.1 | async-start | bytes 1048576 | tf_op jit(solution)/shard_map/all_to_all | solution.py:213
  318.2 309.8 %all-reduce.4.cloned.1.call-start = ((), (), s32[]{:S(2)}) async-start(), calls=%async_computation.4 | async-start | bytes 28311552 | tf_op jit(solution)/shard_map/psum | solution.py:228
  628.0 11.9 %copy-start.1 = (bf16[512,512]{1,0:T(8,128)(2,1)S(1)}, bf16[512,512]{1,0:T(8,128)(2,1)}, u32[]{:S(2)}) copy-start(bf16[512,512]{1,0:T(8,128)(2,1)} %param.19) | copy-start | bytes 1572868
  (8 other events, 20.9 us)
Sparse Core Ops, SparseCore 0:
  34.7 63.3 all-gather.2
  100.4 61.3 all-gather.4
  454.9 173.0 all-reduce.3
where the time goes:
time: 651 us; the launch traced here: 646 us
  waiting for transfers between devices  318 us (49%)
  local copies, waits for them, and re-layouts  125 us (19%)
  matrix products  66.8 us (10%)
  loops' own time  53.8 us (8%)
  other arithmetic  28.5 us (4%)
  blocking collectives  22.1 us (3%)
  starting transfers between devices  17 us (3%)
  between operations  14.7 us (2%)
    psum x1, waiting for transfers between devices, on_device(): conv_total = lax.psum(local_grad, ('clip', 'tile'))  172 us
    all_gather x1, waiting for transfers between devices, on_device(): lax.all_gather(keys_local, 'tile', axis=0, tiled=True)  58.6 us
    all_gather x1, waiting for transfers between devices, on_device(): lax.all_gather(values_local, 'tile', axis=0, tiled=True)  54.9 us
    another operation x1, loops' own time, on_device(): lax.fori_loop(0, tiles * CAP, add_slot, jnp.zeros((frames, rows_dev, cols...  53.8 us
    slice x26, local copies, waits for them, and re-layouts, conv_forward(): padded[offset_t:offset_t + frames, offset_y:offset_y + rows, offset_x:off...  50.3 us
    dot_general x27, matrix products, conv_forward(): jnp.dot(tap, conv_weight[offset_t, offset_y, offset_x], preferred_element...  38.9 us
    dynamic_update_slice x16, local copies, waits for them, and re-layouts, add_slot(): return lax.dynamic_update_slice(grad_map, current + update, start)  24.3 us
    psum x1, blocking collectives, on_device(): lax.psum((jnp.sum(grouped, axis=(0, 2)), jnp.sum(grouped * grouped, axis=...  22.1 us
  transfers between devices with their start and end apart: 7, of which 7 were waited for; matrix products, arithmetic and copies ran while one was open for 3% of the time, Pallas kernels for 0%

commit v1 on v0

v1 whole, which is shorter than its diff:
```python
import functools
import math

import jax
import jax.numpy as jnp
from jax import lax
from jax.experimental import pallas as pl
from jax.experimental.pallas import tpu as pltpu
from jax.sharding import PartitionSpec as P

GROUPS = 32
CROPW = 64
EPSILON = 1e-06
F32 = jnp.float32
BF16 = jnp.bfloat16


def dot(a, b):
    return jnp.dot(a, b, preferred_element_type=F32)


def dot_nt(a, b):
    return lax.dot_general(a, b, (((1,), (1,)), ((), ())), preferred_element_type=F32)


def dot_tn(a, b):
    return lax.dot_general(a, b, (((0,), (0,)), ((), ())), preferred_element_type=F32)


def gelu_parts(z):
    k = math.sqrt(2.0 / math.pi)
    t = jnp.tanh(k * (z + 0.044715 * (z * z * z)))
    return 0.5 * z * (1.0 + t), t


def gelu_slope(z, t):
    k = math.sqrt(2.0 / math.pi)
    return 0.5 * (1.0 + t) + 0.5 * z * (1.0 - t * t) * (k * (1.0 + 3.0 * 0.044715 * (z * z)))


def shift_rows(value, step, cols):
    count = value.shape[0]
    place = lax.broadcasted_iota(jnp.int32, (count, 1), 0) % cols
    if step > 0:
        return jnp.where(place == 0, 0.0, pltpu.roll(value, 1, 0))
    return jnp.where(place == cols - 1, 0.0, pltpu.roll(value, count - 1, 0))


def body(
    tiles, frames, cols, gsum_ref,
    mine_ref, feats_ref, gain_ref, wq_ref, wk_ref, wv_ref, wo_ref, bias_ref, percept_ref,
    lpips_ref, target_ref, owner_ref, frame_ref, col_ref, weight_hbm,
    decoded_ref, hidden_t, grad_ref, dist_ref,
    weight, normed, qs, acc, peak, total, hidden, sem,
):
    mine = mine_ref[0]
    cells = frames * cols
    width = feats_ref.shape[-1]
    outputs = bias_ref.shape[-1]
    fetch = pltpu.make_async_copy(weight_hbm, weight, sem)
    fetch.start()

    def add_tile(i, sums):
        x = feats_ref[i].astype(F32)
        return (
            sums[0] + jnp.sum(x, axis=0, keepdims=True),
            sums[1] + jnp.sum(x * x, axis=0, keepdims=True),
        )

    zero_row = jnp.zeros((1, width), F32)
    first, second = lax.fori_loop(0, tiles, add_tile, (zero_row, zero_row))
    sums = jnp.concatenate([first, second, jnp.zeros((6, width), F32)], axis=0)
    grouped = jnp.dot(sums, gsum_ref[...], precision=lax.Precision.HIGHEST, preferred_element_type=F32)
    count = F32(tiles * cells * (width // GROUPS))
    mean = grouped[0:1] / count
    spread = grouped[1:2] / count - mean * mean
    scale = lax.rsqrt(spread + EPSILON)
    gain = gain_ref[...]

    def normalize(i, _):
        x = feats_ref[i].astype(F32)
        normed[i] = (((x - mean) * scale) * gain).astype(BF16)
        return 0

    lax.fori_loop(0, tiles, normalize, 0)

    factor = 1.0 / math.sqrt(width)

    def row_of(b):
        return jnp.clip(mine + b - 1, 0, tiles - 1)

    def make_queries(b, _):
        q = dot(normed[row_of(b)], wq_ref[...]).astype(BF16)
        here = pl.ds(b * cells, cells)
        qs[here, :] = (dot_nt(q, wk_ref[...]) * factor).astype(BF16)
        acc[here, :] = jnp.zeros((cells, width), F32)
        peak[here, :] = jnp.full((cells, 128), -1e30, F32)
        total[here, :] = jnp.zeros((cells, 128), F32)
        return 0

    lax.fori_loop(0, 3, make_queries, 0)

    def attend(step, _):
        i = step // 3
        here = pl.ds((step % 3) * cells, cells)
        keys = normed[i]
        s = dot_nt(qs[here, :], keys)
        old = peak[here, :]
        new = jnp.maximum(old, jnp.max(s, axis=1, keepdims=True))
        p = jnp.exp(s - new[:, 0:1])
        fade = jnp.exp(old - new)
        part = p[:, 0:128]
        for j in range(1, cells // 128):
            part = part + p[:, j * 128 : (j + 1) * 128]
        peak[here, :] = new
        total[here, :] = total[here, :] * fade + part
        acc[here, :] = acc[here, :] * fade[:, 0:1] + dot(p.astype(BF16), keys)
        return 0

    lax.fori_loop(0, tiles * 3, attend, 0)

    def finish(b, _):
        here = pl.ds(b * cells, cells)
        whole = jnp.sum(total[here, :], axis=1, keepdims=True)
        context = (acc[here, :] / whole).astype(BF16)
        mixed = dot(context, wv_ref[...]).astype(BF16)
        row = feats_ref[row_of(b)].astype(F32) + dot(mixed, wo_ref[...])
        inside = (mine + b >= 1) & (mine + b <= tiles)
        row = jnp.where(inside, row, 0.0)
        hidden[b] = row.astype(BF16)
        hidden_t[b] = row.T.astype(BF16)
        return 0

    lax.fori_loop(0, 3, finish, 0)
    fetch.wait()

    sides = []
    for e in range(3):
        def taps(b, sums, e=e):
            h = hidden[b]
            at = lambda a: weight[(a * 3 + b) * 3 + e]
            return (
                sums[0] + dot(h, at(2)),
                sums[1] + dot(h[: 2 * cols], at(1)),
                sums[2] + dot(h[:cols], at(0)),
            )
        a2, a1, a0 = lax.fori_loop(
            0, 3, taps,
            (jnp.zeros((cells, outputs), F32), jnp.zeros((2 * cols, outputs), F32), jnp.zeros((cols, outputs), F32)),
        )
        sides.append(a2 + jnp.concatenate([a1[:cols], a1], axis=0) + jnp.concatenate([a0, a0, a0], axis=0))
    made = shift_rows(sides[0], 1, cols) + sides[1] + shift_rows(sides[2], -1, cols) + bias_ref[...]
    made = made.astype(BF16)
    decoded_ref[...] = made

    table = percept_ref[...]
    lw = lpips_ref[...]
    z = dot(made, table)
    m, t = gelu_parts(z)
    s = lax.rsqrt(jnp.mean(m * m, axis=-1, keepdims=True) + EPSILON)
    zt = dot(target_ref[...], table)
    mt, _ = gelu_parts(zt)
    st = lax.rsqrt(jnp.mean(mt * mt, axis=-1, keepdims=True) + EPSILON)
    gap = m * s - mt * st
    weighted = gap * lw
    apart = jnp.sum(weighted * gap, axis=-1, keepdims=True)
    up = weighted * (2.0 / CROPW)
    dm = up * s - m * (s * s * s) * (jnp.sum(up * m, axis=-1, keepdims=True) / outputs)
    dz = dm * gelu_slope(z, t)
    high = dz.astype(BF16)
    low = (dz - high.astype(F32)).astype(BF16)
    pull = (dot_nt(high, table) + dot_nt(low, table)).astype(BF16).astype(F32)

    place = lax.broadcasted_iota(jnp.int32, (cols, 1), 0)
    col = col_ref[...]
    covers = (place >= col) & (place < col + CROPW) & (owner_ref[...] == mine)
    distance = jnp.zeros((1, col.shape[1]), F32)
    for f in range(frames):
        cover = (covers & (frame_ref[...] == f)).astype(F32)
        rows = slice(f * cols, (f + 1) * cols)
        distance = distance + jnp.sum(cover * apart[rows], axis=0, keepdims=True)
        grad_ref[rows, :] = (pull[rows] * jnp.sum(cover, axis=1, keepdims=True)).astype(BF16)
    dist_ref[...] = jnp.broadcast_to(distance / CROPW, dist_ref.shape)


def chip_place():
    clip = lax.axis_index("clip")
    tile = lax.axis_index("tile")
    return (tile // 2, clip // 4, (tile % 2) * 2 + (clip // 2) % 2), clip % 2


def device_at(place, core):
    x, y, z = place
    return (y * 4 + (z % 2) * 2 + core, x * 2 + z // 2)


def on_axis(place, axis, position):
    moved = list(place)
    moved[axis] = lax.rem(position + 4, 4)
    return tuple(moved)


def grad_sum(
    frames, cols, hidden_t, grad_hbm, dist_ref, out_ref, dist_out,
    own_h, other_h, own_g, other_g, rhs, part, left1, right1, comb, got, red1, got2, got3, quarter,
    dist_row, dist_pair, send, recv, local, swap_send, swap_recv, dist_send, dist_recv,
):
    place, core = chip_place()
    cells = frames * cols
    outputs = grad_hbm.shape[1]
    half = own_h.shape[1]
    quarter_rows = red1.shape[1]
    half_rows = quarter_rows // 2
    piece = quarter_rows // 4
    partner = device_at(place, 1 - core)

    def peer(axis, step):
        return device_at(on_axis(place, axis, place[axis] + step), core)

    barrier = pltpu.get_barrier_semaphore()
    peers = [peer(axis, step) for axis in range(3) for step in (1, 2, 3)] + [partner]
    for other in peers:
        pl.semaphore_signal(barrier, inc=1, device_id=other, device_id_type=pl.DeviceIdType.MESH)
    own1 = pltpu.make_async_copy(hidden_t.at[:, pl.ds(core * half, half)], own_h, local.at[0])
    own2 = pltpu.make_async_copy(grad_hbm, own_g, local.at[1])
    own1.start()
    own2.start()
    pl.semaphore_wait(barrier, len(peers))

    def remote(src, dst, sems, rsems, index, target):
        return pltpu.make_async_remote_copy(
            src_ref=src, dst_ref=dst, send_sem=sems.at[index], recv_sem=rsems.at[index],
            device_id=target, device_id_type=pl.DeviceIdType.MESH,
        )

    swap_h = remote(hidden_t.at[:, pl.ds((1 - core) * half, half)], other_h, swap_send, swap_recv, 0, partner)
    swap_g = remote(grad_hbm, other_g, swap_send, swap_recv, 1, partner)
    swap_g.start()
    swap_h.start()
    row_copies = []
    for step in (1, 2, 3):
        copy = remote(dist_ref, dist_row.at[step - 1], dist_send, dist_recv, step - 1, peer(0, step))
        copy.start()
        row_copies.append(copy)

    own1.wait()
    own2.wait()
    swap_g.wait()
    swap_h.wait()

    def ring_copy(p, kind):
        m = place[p]
        rows = lambda q, h: pl.ds(pl.multiple_of(lax.rem(q + 4, 4) * quarter_rows + h * half_rows, 16), half_rows)
        source, target, step = {
            0: (part.at[p, rows(m + 2, 0)], left1.at[p], 1),
            1: (part.at[p, rows(m + 2, 1)], right1.at[p], 3),
            2: (part.at[p, rows(m + 1, 1)], got.at[p, 0, pl.ds(half_rows, half_rows)], 1),
            3: (part.at[p, rows(m - 1, 0)], got.at[p, 1, pl.ds(0, half_rows)], 3),
            4: (comb.at[p, 0], got.at[p, 0, pl.ds(0, half_rows)], 1),
            5: (comb.at[p, 1], got.at[p, 1, pl.ds(half_rows, half_rows)], 3),
        }[kind]
        return remote(source, target, send, recv, p * 27 + kind, peer(p, step))

    g_own = [own_g[f * cols : (f + 1) * cols].astype(F32) for f in range(frames)]
    g_other = [other_g[f * cols : (f + 1) * cols].astype(F32) for f in range(frames)]
    mixes = (
        lambda g: [g[0] + g[1] + g[2]],
        lambda g: [g[0] + g[1], g[2]],
        lambda g: g,
    )
    ring = [[ring_copy(p, kind) for kind in range(6)] for p in range(3)]
    for p in range(3):
        depth = (p + 1) * cols
        both = jnp.concatenate(mixes[p](g_own) + mixes[p](g_other), axis=0)
        rhs[: 2 * depth] = jnp.concatenate(
            [shift_rows(both, -1, cols), both, shift_rows(both, 1, cols)], axis=1
        ).astype(BF16)

        def write(b, _, p=p, depth=depth):
            lhs = jnp.concatenate([own_h[b, :, :depth], other_h[b, :, :depth]], axis=1)
            for e in range(3):
                base = pl.multiple_of((b * 3 + e) * half, half)
                part[p, pl.ds(base, half), :] = dot(
                    lhs, rhs[: 2 * depth, e * outputs : (e + 1) * outputs]
                ).astype(BF16)
            return 0

        lax.fori_loop(0, 3, write, 0)
        for kind in range(4):
            ring[p][kind].start()

    total = dist_ref[...]
    for copy in row_copies:
        copy.wait()
    by_step = [dist_ref[...]] + [dist_row[i] for i in range(3)]
    total = by_step[0] + by_step[1] + by_step[2] + by_step[3]
    dist_pair[0] = total
    pair = remote(dist_pair.at[0], dist_pair.at[1], dist_send, dist_recv, 3, peer(2, 2))
    pair.start()

    for p in range(3):
        m = place[p]
        for side, kind, arrived, q, h in ((0, 0, left1, m + 1, 0), (1, 1, right1, m - 1, 1)):
            ring[p][kind].wait_recv()
            rows = pl.ds(pl.multiple_of(lax.rem(q + 4, 4) * quarter_rows + h * half_rows, 16), half_rows)
            comb[p, side] = (part[p, rows, :].astype(F32) + arrived[p].astype(F32)).astype(BF16)
            ring[p][4 + side].start()
    pair.wait()
    mine = lax.axis_index("tile")
    count = dist_out.shape[1]
    pick = lax.broadcasted_iota(jnp.int32, (dist_ref.shape[1], count), 0) == (
        mine * count + lax.broadcasted_iota(jnp.int32, (dist_ref.shape[1], count), 1)
    )
    dist_out[...] = jnp.dot(
        dist_pair[0] + dist_pair[1], pick.astype(F32), precision=lax.Precision.HIGHEST, preferred_element_type=F32
    )[0:1]

    second = []
    for p in range(3):
        axis = (p + 1) % 3
        for kind in (2, 3, 4, 5):
            ring[p][kind].wait_recv()
        own = part[p, pl.ds(pl.multiple_of(place[p] * quarter_rows, 16), quarter_rows), :].astype(F32)
        red1[p] = (own + got[p, 0].astype(F32) + got[p, 1].astype(F32)).astype(BF16)
        copies = []
        for step in (1, 2, 3):
            to = lax.rem(place[axis] + step, 4)
            copy = remote(
                red1.at[p, pl.ds(pl.multiple_of(to * piece, 16), piece)], got2.at[p, step - 1],
                send, recv, p * 27 + 5 + step, peer(axis, step),
            )
            copy.start()
            copies.append(copy)
        second.append(copies)

    third = []
    for p in range(3):
        axis = (p + 2) % 3
        here = place[(p + 1) % 3]
        for copy in second[p]:
            copy.wait_recv()
        piece_sum = red1[p, pl.ds(pl.multiple_of(here * piece, 16), piece), :].astype(F32)
        for i in range(3):
            piece_sum = piece_sum + got2[p, i].astype(F32)
        got3[p, place[axis]] = piece_sum.astype(BF16)
        copies = []
        for step in (1, 2, 3):
            slot = got3.at[p, place[axis]]
            copy = remote(slot, slot, send, recv, p * 27 + 8 + step, peer(axis, step))
            copy.start()
            copies.append(copy)
        third.append(copies)

    fourth = []
    for p in range(3):
        axis = (p + 1) % 3
        for copy in third[p]:
            copy.wait_recv()
        whole = got3[p, 0].astype(F32)
        for i in range(1, 4):
            whole = whole + got3[p, i].astype(F32)
        rows = pl.ds(pl.multiple_of(place[axis] * piece, 16), piece)
        quarter[p, rows, :] = whole.astype(BF16)
        copies = []
        for step in (1, 2, 3):
            slot = quarter.at[p, rows]
            copy = remote(slot, slot, send, recv, p * 27 + 11 + step, peer(axis, step))
            copy.start()
            copies.append(copy)
        fourth.append(copies)

    def out_rows(p, q, h, count=1):
        start = pl.multiple_of(lax.rem(q + 4, 4) * quarter_rows + h * half_rows, 16)
        return out_ref.at[core, p, pl.ds(start, half_rows * count)]

    fifth, to_core, stored = [], [], []
    for p in range(3):
        m = place[p]
        for copy in fourth[p]:
            copy.wait_recv()
        copies = {}
        for kind, h, step in ((0, 0, 1), (1, 1, 3), (2, 1, 1), (3, 0, 3)):
            copies[kind] = remote(
                quarter.at[p, pl.ds(h * half_rows, half_rows)], out_rows(p, m, h), send, recv, p * 27 + 15 + kind,
                peer(p, step),
            )
            copies[kind].start()
        fifth.append(copies)
        across = remote(quarter.at[p], out_rows(p, m, 0, 2), send, recv, p * 27 + 21, partner)
        across.start()
        to_core.append(across)
        store = pltpu.make_async_copy(quarter.at[p], out_rows(p, m, 0, 2), local.at[2 + p])
        store.start()
        stored.append(store)
    forward = []
    for p in range(3):
        m = place[p]
        for kind, q, h, step in ((0, m - 1, 0, 1), (1, m + 1, 1, 3)):
            fifth[p][kind].wait_recv()
            rows = out_rows(p, q, h)
            copy = remote(rows, rows, send, recv, p * 27 + 19 + kind, peer(p, step))
            copy.start()
            forward.append(copy)
    for p in range(3):
        m = place[p]
        for kind, q, index in ((2, m - 1, 22), (3, m + 1, 23)):
            fifth[p][kind].wait_recv()
            rows = out_rows(p, q, 0, 2)
            copy = remote(rows, rows, send, recv, p * 27 + index, partner)
            copy.start()
            to_core.append(copy)
    for p in range(3):
        m = place[p]
        for side in range(2):
            forward[p * 2 + side].wait_recv()
            rows = out_rows(p, m + 2, side)
            copy = remote(rows, rows, send, recv, p * 27 + 24 + side, partner)
            copy.start()
            to_core.append(copy)
    for copy in to_core:
        copy.wait()
    for copy in stored:
        copy.wait()
    for p in range(3):
        for kind in range(6):
            ring[p][kind].wait_send()
        for copy in second[p] + third[p] + fourth[p] + [fifth[p][kind] for kind in range(4)]:
            copy.wait_send()
    for copy in forward:
        copy.wait_send()


def on_device(
    features, target, gn_gain, attn_query, attn_key, attn_value, attn_out, conv_weight, conv_bias,
    percept, lpips_weight, crop_owner, crop_frame, crop_col,
):
    tiles = lax.axis_size("tile")
    mine = lax.axis_index("tile").astype(jnp.int32)
    frames, rows_dev, cols, width = features.shape[1:]
    outputs = conv_weight.shape[-1]
    cells = frames * rows_dev * cols
    taps = 27
    group = width // GROUPS
    lane = jnp.arange(width) // group
    gsum = (lane[:, None] == lane[None, :]).astype(F32)
    gathered = lax.all_gather(features.reshape(cells, width), "tile", axis=0)
    vmem = pl.BlockSpec(memory_space=pltpu.VMEM)
    half = width // 2
    part_rows = taps // 3 * half
    quarter_rows = part_rows // 4
    crops = crop_col.shape[1]
    decoded, hidden_t, grad, dist = pl.pallas_call(
        functools.partial(body, tiles, frames, cols),
        in_specs=[vmem, pl.BlockSpec(memory_space=pltpu.SMEM)] + [vmem] * 13 + [pl.BlockSpec(memory_space=pl.ANY)],
        out_specs=[vmem] * 4,
        out_shape=[
            jax.ShapeDtypeStruct((cells, outputs), BF16),
            jax.ShapeDtypeStruct((3, width, cells), BF16),
            jax.ShapeDtypeStruct((cells, outputs), BF16),
            jax.ShapeDtypeStruct((8, crops), F32),
        ],
        scratch_shapes=[
            pltpu.VMEM((taps, width, outputs), BF16),
            pltpu.VMEM((tiles, cells, width), BF16),
            pltpu.VMEM((3 * cells, width), BF16),
            pltpu.VMEM((3 * cells, width), F32),
            pltpu.VMEM((3 * cells, 128), F32),
            pltpu.VMEM((3 * cells, 128), F32),
            pltpu.VMEM((3, cells, width), BF16),
            pltpu.SemaphoreType.DMA,
        ],
        compiler_params=pltpu.CompilerParams(vmem_limit_bytes=60 * 1024 * 1024),
        cost_estimate=pl.CostEstimate(flops=12_000_000_000, bytes_accessed=14_000_000, transcendentals=4_000_000),
        name="decoder_window",
    )(
        gsum, mine.reshape(1), gathered, gn_gain[None, :], attn_query, attn_key, attn_value, attn_out,
        conv_bias[None, :], percept, lpips_weight[None, :], target.reshape(cells, outputs),
        crop_owner.reshape(1, -1), crop_frame, crop_col, conv_weight.reshape(taps, width, outputs),
    )
    hbm = pl.BlockSpec(memory_space=pl.ANY)
    summed, distances = pl.pallas_call(
        functools.partial(grad_sum, frames, cols),
        in_specs=[hbm, hbm, vmem],
        out_specs=[hbm, vmem],
        out_shape=[
            jax.ShapeDtypeStruct((2, 3, part_rows, outputs), BF16),
            jax.ShapeDtypeStruct((1, crops // tiles), F32),
        ],
        scratch_shapes=[
            pltpu.VMEM((3, half, cells), BF16),
            pltpu.VMEM((3, half, cells), BF16),
            pltpu.VMEM((cells, outputs), BF16),
            pltpu.VMEM((cells, outputs), BF16),
            pltpu.VMEM((2 * cells, 3 * outputs), BF16),
            pltpu.VMEM((3, part_rows, outputs), BF16),
            pltpu.VMEM((3, quarter_rows // 2, outputs), BF16),
            pltpu.VMEM((3, quarter_rows // 2, outputs), BF16),
            pltpu.VMEM((3, 2, quarter_rows // 2, outputs), BF16),
            pltpu.VMEM((3, 2, quarter_rows, outputs), BF16),
            pltpu.VMEM((3, quarter_rows, outputs), BF16),
            pltpu.VMEM((3, 3, quarter_rows // 4, outputs), BF16),
            pltpu.VMEM((3, 4, quarter_rows // 4, outputs), BF16),
            pltpu.VMEM((3, quarter_rows, outputs), BF16),
            pltpu.VMEM((3, 8, crops), F32),
            pltpu.VMEM((2, 8, crops), F32),
            pltpu.SemaphoreType.DMA((81,)),
            pltpu.SemaphoreType.DMA((81,)),
            pltpu.SemaphoreType.DMA((5,)),
            pltpu.SemaphoreType.DMA((2,)),
            pltpu.SemaphoreType.DMA((2,)),
            pltpu.SemaphoreType.DMA((4,)),
            pltpu.SemaphoreType.DMA((4,)),
        ],
        compiler_params=pltpu.CompilerParams(
            collective_id=1, has_side_effects=True, vmem_limit_bytes=50 * 1024 * 1024
        ),
        cost_estimate=pl.CostEstimate(flops=3_000_000_000, bytes_accessed=14_000_000, transcendentals=0),
        name="grad_sum",
    )(hidden_t, grad, dist)
    conv_total = summed.reshape(2, taps, half, outputs).transpose(1, 0, 2, 3).astype(F32).reshape(conv_weight.shape)
    return (decoded.reshape(1, frames, rows_dev, cols, outputs), conv_total, distances)


def solution(mesh):
    return jax.shard_map(
        on_device,
        mesh=mesh,
        in_specs=(
            P("clip", None, "tile", None, None),
            P("clip", None, "tile", None, None),
            P(), P(), P(), P(), P(), P(), P(), P(), P(),
            P("clip", None, None),
            P("clip", None),
            P("clip", None),
        ),
        out_specs=(P("clip", None, "tile", None, None), P(), P("clip", "tile")),
        check_vma=False,
    )
```

time: 651 us -> 201 us (0.31)
  waiting for transfers between devices: 318 us -> 67.9 us
  local copies, waits for them, and re-layouts: 125 us -> 15.3 us
  Pallas kernels: 0 us -> 92.9 us
  matrix products: 66.8 us -> 0 us
  loops' own time: 53.8 us -> 0 us
  blocking collectives: 22.1 us -> 0 us
  other arithmetic: 28.5 us -> 11.1 us
  starting transfers between devices: 17 us -> 0.04 us
    psum x1 -> x0, waiting for transfers between devices: 172 us -> none  [on_device(): conv_total = lax.psum(local_grad, ('clip', 'tile'))]
    pallas_call x0 -> x2, Pallas kernels: none -> 92.9 us  [the longest x1 53.1 us: on_device(): pl.pallas_call(functools.partial(grad_sum, frames, cols), in_specs=[hbm,...]
    dot_general x61 -> x0, matrix products: 66.8 us -> none  [the longest x27 38.9 us: conv_forward(): jnp.dot(tap, conv_weight[offset_t, offset_y, offset_x], preferred_element...]
    another operation x1 -> x0, loops' own time: 53.8 us -> none  [on_device(): lax.fori_loop(0, tiles * CAP, add_slot, jnp.zeros((frames, rows_dev, cols...]
    slice x26 -> x0, local copies, waits for them, and re-layouts: 50.3 us -> none  [conv_forward(): padded[offset_t:offset_t + frames, offset_y:offset_y + rows, offset_x:off...]
    all_gather x2 -> x1, waiting for transfers between devices: 113 us -> 67.2 us  [on_device(): gathered = lax.all_gather(features.reshape(cells, width), 'tile', axis=0)]
    all_to_all x2 -> x0, waiting for transfers between devices: 24.3 us -> none  [the longest x1 15.3 us: on_device(): lax.all_to_all(packed, 'tile', split_axis=0, concat_axis=0, tiled=True)]
    dynamic_update_slice x16 -> x0, local copies, waits for them, and re-layouts: 24.3 us -> none  [add_slot(): return lax.dynamic_update_slice(grad_map, current + update, start)]
  transfers between devices with their start and end apart: 7 -> 1, of which waited for: 7 -> 1; matrix products, arithmetic and copies ran while one was open for 3% -> 1% of each run, Pallas kernels for 0% -> 0%
where the time goes in v1:
time: 201 us
  Pallas kernels  92.9 us (46%)
  waiting for transfers between devices  67.9 us (34%)
  local copies, waits for them, and re-layouts  15.3 us (8%)
  between operations  14.1 us (7%)
  other arithmetic  11.1 us (6%)
    all_gather x1, waiting for transfers between devices, on_device(): gathered = lax.all_gather(features.reshape(cells, width), 'tile', axis=0)  67.2 us
    pallas_call x1, Pallas kernels, on_device(): pl.pallas_call(functools.partial(grad_sum, frames, cols), in_specs=[hbm,...  53.1 us
    pallas_call x1, Pallas kernels, on_device(): pl.pallas_call(functools.partial(body, tiles, frames, cols), in_specs=[vm...  39.7 us
    reshape x1, local copies, waits for them, and re-layouts, on_device(): summed.reshape(2, taps, half, outputs).transpose(1, 0, 2, 3).astype(F32)  11.9 us
    reshape x1, other arithmetic, on_device(): summed.reshape(2, taps, half, outputs).transpose(1, 0, 2, 3).astype(F32)  9.93 us
  transfers between devices with their start and end apart: 1, of which 1 were waited for; matrix products, arithmetic and copies ran while one was open for 1% of the time, Pallas kernels for 0%

profile of v1, /device:TPU:1, one launch (start us, length us, event | category | flops | bytes accessed | tf_op | source)
XLA Modules:
  0.0 201.2 jit_solution(8829410332041342710)
XLA Ops:
  7.2 0.0 all-gather.2.cloned.1.call-start
  7.2 0.7 all-gather.2.cloned.1.call-update
  7.9 1.1 compare_convert_fusion.gsum_ref
  9.0 67.2 %all-gather.2.cloned.1.call-done.feats_ref = bf16[8,384,512]{2,1,0:T(8,128)(2,1)} async-done(((bf16[1,384,512]{2,1,0:T(8,128)(2,1)}), bf16[8,384,512]{2,1,0:T(8,128)(2,1)}) %all-gather.2.cloned.1.call-update) | async-done | bytes 3145744 | tf_op jit(solution)/shard_map/all_gather | solution.py:446
  76.2 39.7 %decoder_window.1 = (bf16[384,256]{1,0:T(8,128)(2,1)}, bf16[3,512,384]{2,1,0:T(8,128)(2,1)}, bf16[384,256]{1,0:T(8,128)(2,1)}, f32[8,64]{1,0:T(8,128)}) custom-call(f32[512,512]{1,0:T(8,128)} %compare_convert_fusion.gsum_ref, s32[1]{0:T(128)} %bitcast.mine_ref, bf16[8,384,512]{2,1,0:T(8,128)(2,1)} %all-gather.2.cloned.1.call-done.feats_ref, ...), custom_call_target="tpu_custom_call" | custom-call | flops 12000000000 | bytes 14000000 | tf_op jit(solution)/shard_map/decoder_window/pallas_call | solution.py:452
  116.0 0.0 copy-start
  116.0 1.3 copy-done
  117.3 0.0 copy-start.1
  117.3 0.9 copy-done.1
  118.2 0.0 copy-start.2
  118.2 0.7 copy-done.2
  118.9 53.1 %grad_sum.1 = (bf16[2,3,2304,256]{3,2,1,0:T(8,128)(2,1)}, f32[1,8]{1,0:T(1,128)S(1)}) custom-call(bf16[3,512,384]{2,1,0:T(8,128)(2,1)S(1)} %copy-done, bf16[384,256]{1,0:T(8,128)(2,1)S(1)} %copy-done.1, f32[8,64]{1,0:T(8,128)S(1)} %copy-done.2), custom_call_target="tpu_custom_call" | custom-call | flops 3000000000 | bytes 14000000 | tf_op jit(solution)/shard_map/grad_sum/pallas_call | solution.py:481
  172.0 9.9 %convert_bitcast_fusion = f32[27,2,256,256]{3,2,0,1:T(8,128)} fusion(bf16[2,27,256,256]{3,2,1,0:T(8,128)(2,1)} %bitcast.17), kind=kLoop, calls=%fused_computation | loop fusion | flops 3538944 | bytes 21233664 | tf_op jit(solution)/shard_map/reshape | solution.py:520
  181.9 11.9 %copy.19 = f32[27,2,256,256]{3,2,1,0:T(8,128)} copy(f32[27,2,256,256]{3,2,0,1:T(8,128)} %convert_bitcast_fusion) | data formatting | bytes 28311552 | tf_op jit(solution)/shard_map/reshape | solution.py:520
  193.9 0.5 copy.22
  (1 shorter events, 0.0 us)
Async XLA Ops:
  7.2 69.1 %all-gather.2.cloned.1.call-start = ((), (), s32[]{:S(2)}) async-start(), calls=%async_computation | async-start | bytes 3538944 | tf_op jit(solution)/shard_map/all_gather | solution.py:446
  116.0 1.3 copy-start
  117.3 0.9 copy-start.1
  118.2 0.7 copy-start.2
Sparse Core Ops, SparseCore 0:
  10.3 65.8 all-gather.1

commit v2 on v0

v2 whole, which is shorter than its diff:
```python
import functools
import math

import jax
import jax.numpy as jnp
from jax import lax
from jax.experimental import pallas as pl
from jax.experimental.pallas import tpu as pltpu
from jax.sharding import PartitionSpec as P

GROUPS = 32
CROPW = 64
EPSILON = 1e-06
F32 = jnp.float32
BF16 = jnp.bfloat16


def dot(a, b):
    return jnp.dot(a, b, preferred_element_type=F32)


def dot_nt(a, b):
    return lax.dot_general(a, b, (((1,), (1,)), ((), ())), preferred_element_type=F32)


def dot_tn(a, b):
    return lax.dot_general(a, b, (((0,), (0,)), ((), ())), preferred_element_type=F32)


def gelu_parts(z):
    k = math.sqrt(2.0 / math.pi)
    t = jnp.tanh(k * (z + 0.044715 * (z * z * z)))
    return 0.5 * z * (1.0 + t), t


def gelu_slope(z, t):
    k = math.sqrt(2.0 / math.pi)
    return 0.5 * (1.0 + t) + 0.5 * z * (1.0 - t * t) * (k * (1.0 + 3.0 * 0.044715 * (z * z)))


def shift_rows(value, step, cols):
    count = value.shape[0]
    place = lax.broadcasted_iota(jnp.int32, (count, 1), 0) % cols
    if step > 0:
        return jnp.where(place == 0, 0.0, pltpu.roll(value, 1, 0))
    return jnp.where(place == cols - 1, 0.0, pltpu.roll(value, count - 1, 0))


def chip_place():
    clip = lax.axis_index("clip")
    tile = lax.axis_index("tile")
    return (tile // 2, clip // 4, (tile % 2) * 2 + (clip // 2) % 2), clip % 2


def device_at(place, core):
    x, y, z = place
    return (y * 4 + (z % 2) * 2 + core, x * 2 + z // 2)


def on_axis(place, axis, position):
    moved = list(place)
    moved[axis] = lax.rem(position + 4, 4)
    return tuple(moved)


def decoder_window(
    tiles, frames, cols,
    features, target_ref, gain_ref, wq_ref, wk_ref, wv_ref, wo_ref, bias_ref, percept_ref, lpips_ref,
    owner_ref, frame_ref, col_ref, weight_hbm,
    decoded_ref, out_ref, dist_out,
    weight, feats, normed, stats, qs, acc, peak, total, hidden, hidden_t, other_h, own_g, other_g, rhs,
    part, left1, right1, comb, got, red1, got2, got3, quarter, dist_row, dist_pair,
    gather_send, gather_recv, stat_send, stat_recv, swap_send, swap_recv, dist_send, dist_recv, send, recv, local,
):
    place, core = chip_place()
    clip = lax.axis_index("clip")
    mine = lax.axis_index("tile")
    x, side = mine // 2, mine % 2
    cells = frames * cols
    width = feats.shape[-1]
    outputs = bias_ref.shape[-1]
    half = width // 2
    cut = cells // 2

    def tile_at(step, other):
        return lax.rem(x + step + 4, 4) * 2 + (side + other) % 2

    def peer(axis, step):
        return device_at(on_axis(place, axis, place[axis] + step), core)

    def remote(src, dst, sems, rsems, index, target):
        copy = pltpu.make_async_remote_copy(
            src_ref=src, dst_ref=dst, send_sem=sems.at[index], recv_sem=rsems.at[index],
            device_id=target, device_id_type=pl.DeviceIdType.MESH,
        )
        copy.start()
        return copy

    own, left, right, opposite = (tile_at(step, 0) for step in (0, -1, 1, 2))
    partner, left2, right2, opposite2 = (tile_at(step, 1) for step in (0, -1, 1, 2))
    far = jnp.where(side == 0, left2, right2)
    near = jnp.where(side == 0, right2, left2)
    sibling = device_at(place, 1 - core)

    barrier = pltpu.get_barrier_semaphore()
    peers = [(clip, lax.rem(mine + step, tiles)) for step in range(1, tiles)]
    peers += [peer(1, 1), peer(1, 2), peer(1, 3), peer(2, 1), peer(2, 3), sibling]
    for other in peers:
        pl.semaphore_signal(barrier, inc=1, device_id=other, device_id_type=pl.DeviceIdType.MESH)
    load = pltpu.make_async_copy(features, feats.at[own], local.at[0])
    load.start()
    fetch = pltpu.make_async_copy(weight_hbm, weight, local.at[1])
    fetch.start()

    load.wait()
    wide = feats[own].astype(F32)
    stats[own] = jnp.concatenate(
        [jnp.sum(wide, axis=0, keepdims=True), jnp.sum(wide * wide, axis=0, keepdims=True), jnp.zeros((6, width), F32)],
        axis=0,
    )
    pl.semaphore_wait(barrier, len(peers))
    told = [
        remote(stats.at[own], stats.at[own], stat_send, stat_recv, step, peers[step]) for step in range(tiles - 1)
    ]

    def pass_on(index, unit, h, to):
        rows = feats.at[unit, pl.ds(h * cut, cut)]
        return remote(rows, rows, gather_send, gather_recv, index, (clip, to))

    links = {}
    links["z0"] = pass_on(0, own, 0, partner)
    links["l0"] = pass_on(1, own, 0, right)
    links["r1"] = pass_on(2, own, 1, left)
    links["z1"] = pass_on(3, own, 1, partner)
    links["l1"] = pass_on(4, own, 1, right)
    links["r0"] = pass_on(5, own, 0, left)

    lane = lax.broadcasted_iota(jnp.int32, (width, width), 0) // (width // GROUPS)
    same = (lane == lax.broadcasted_iota(jnp.int32, (width, width), 1) // (width // GROUPS)).astype(BF16)
    for copy in told:
        copy.wait_recv()
    sums = stats[0]
    for i in range(1, tiles):
        sums = sums + stats[i]
    pieces, rest = [], sums
    for _ in range(3):
        pieces.append(rest.astype(BF16))
        rest = rest - pieces[-1].astype(F32)
    grouped = dot(pieces[0], same) + dot(pieces[1], same) + dot(pieces[2], same)
    count = F32(tiles * cells * (width // GROUPS))
    mean = grouped[0:1] / count
    spread = grouped[1:2] / count - mean * mean
    scale = lax.rsqrt(spread + EPSILON)
    gain = gain_ref[...]
    factor = math.log2(math.e) / math.sqrt(width)

    def normalize(slot, unit):
        normed[slot * cells : (slot + 1) * cells, :] = (((feats[unit].astype(F32) - mean) * scale) * gain).astype(BF16)

    def make_queries(role, slot):
        q = dot(normed[slot * cells : (slot + 1) * cells, :], wq_ref[...]).astype(BF16)
        qs[role * cells : (role + 1) * cells, :] = (dot_nt(q, wk_ref[...]) * factor).astype(BF16)

    def attend(roles, slots, first):
        here = slice(roles[0] * cells, roles[1] * cells)
        keys = normed[slots[0] * cells : slots[1] * cells, :]
        s = dot_nt(qs[here, :], keys)
        groups = [s[:, j : j + 128] for j in range(0, s.shape[1], 128)]
        top = jnp.max(functools.reduce(jnp.maximum, groups), axis=1, keepdims=True)
        new = jnp.broadcast_to(top, (s.shape[0], 128)) if first else jnp.maximum(peak[here, :], top)
        raised = [jnp.exp2(group - new) for group in groups]
        lanes = functools.reduce(jnp.add, raised)
        out = dot(jnp.concatenate([group.astype(BF16) for group in raised], axis=1), keys)
        if first:
            total[here, :] = lanes
            acc[here, :] = out
        else:
            fade = jnp.exp2(peak[here, :] - new)
            total[here, :] = total[here, :] * fade + lanes
            for j in range(0, width, 128):
                acc[here, j : j + 128] = acc[here, j : j + 128] * fade + out[:, j : j + 128]
        peak[here, :] = new

    normalize(0, own)
    make_queries(0, 0)
    links["l0"].wait_recv()
    links["o0"] = pass_on(6, left, 0, right)
    links["r1"].wait_recv()
    links["o1"] = pass_on(7, right, 1, left)
    links["z0"].wait_recv()
    links["l2"] = pass_on(8, partner, 0, right)
    links["z1"].wait_recv()
    links["r3"] = pass_on(9, partner, 1, left)
    links["l3"] = pass_on(10, partner, 1, right)
    links["r2"] = pass_on(11, partner, 0, left)
    normalize(1, partner)
    make_queries(1, 1)
    links["l1"].wait_recv()
    links["r0"].wait_recv()
    normalize(2, left)
    normalize(3, right)
    attend((0, 2), (0, 4), True)
    links["o0"].wait_recv()
    links["o1"].wait_recv()
    normalize(4, opposite)
    links["l2"].wait_recv()
    links["p0"] = pass_on(12, left2, 0, right)
    links["r3"].wait_recv()
    links["p1"] = pass_on(13, right2, 1, left)
    links["l3"].wait_recv()
    links["r2"].wait_recv()
    normalize(5, far)
    normalize(6, near)
    make_queries(2, 5)
    attend((2, 3), (0, 4), True)
    attend((0, 3), (4, 6), False)
    links["p0"].wait_recv()
    links["p1"].wait_recv()
    normalize(7, opposite2)
    attend((0, 3), (6, 8), False)

    def choose(i, values):
        chosen = values[0]
        for j in range(1, len(values)):
            chosen = jnp.where(i == j, values[j], chosen)
        return chosen

    def finish(role, _):
        here = pl.ds(pl.multiple_of(role * cells, cells), cells)
        unit = choose(role, [own, partner, far])
        b = choose(role, [1, 2 - 2 * side, 2 * side])
        whole = jnp.sum(total[here, :], axis=1, keepdims=True)
        context = (acc[here, :] / whole).astype(BF16)
        mixed = dot(context, wv_ref[...]).astype(BF16)
        row = feats[unit].astype(F32) + dot(mixed, wo_ref[...])
        inside = (mine + b >= 1) & (mine + b <= tiles)
        row = jnp.where(inside, row, 0.0)
        hidden[b] = row.astype(BF16)
        hidden_t[b] = row.T.astype(BF16)
        return 0

    lax.fori_loop(0, 3, finish, 0)
    swap_h = remote(
        hidden_t.at[:, pl.ds(pl.multiple_of((1 - core) * half, half), half)], other_h, swap_send, swap_recv, 0, sibling
    )
    fetch.wait()

    sides = []
    for e in range(3):
        a2, a1, a0 = (
            sum(
                dot(hidden[b, : (a + 1) * cols, :], weight[(a * 3 + b) * 3 + e]) for b in range(3)
            )
            for a in (2, 1, 0)
        )
        sides.append(a2 + jnp.concatenate([a1[:cols], a1], axis=0) + jnp.concatenate([a0, a0, a0], axis=0))
    made = shift_rows(sides[0], 1, cols) + sides[1] + shift_rows(sides[2], -1, cols) + bias_ref[...]
    made = made.astype(BF16)
    decoded_ref[...] = made

    table = percept_ref[...]
    lw = lpips_ref[...]
    z = dot(made, table)
    m, t = gelu_parts(z)
    s = lax.rsqrt(jnp.mean(m * m, axis=-1, keepdims=True) + EPSILON)
    zt = dot(target_ref[...], table)
    mt, _ = gelu_parts(zt)
    st = lax.rsqrt(jnp.mean(mt * mt, axis=-1, keepdims=True) + EPSILON)
    gap = m * s - mt * st
    weighted = gap * lw
    apart = jnp.sum(weighted * gap, axis=-1, keepdims=True)
    up = weighted * (2.0 / CROPW)
    dm = up * s - m * (s * s * s) * (jnp.sum(up * m, axis=-1, keepdims=True) / outputs)
    dz = dm * gelu_slope(z, t)
    high = dz.astype(BF16)
    low = (dz - high.astype(F32)).astype(BF16)
    pull = (dot_nt(high, table) + dot_nt(low, table)).astype(BF16).astype(F32)

    spot = lax.broadcasted_iota(jnp.int32, (cols, 1), 0)
    col = col_ref[...]
    covers = (spot >= col) & (spot < col + CROPW) & (owner_ref[...] == mine)
    distance = jnp.zeros((1, col.shape[1]), F32)
    for f in range(frames):
        cover = (covers & (frame_ref[...] == f)).astype(F32)
        rows = slice(f * cols, (f + 1) * cols)
        distance = distance + jnp.sum(cover * apart[rows], axis=0, keepdims=True)
        own_g[rows, :] = (pull[rows] * jnp.sum(cover, axis=1, keepdims=True)).astype(BF16)
    dist_row[3] = jnp.broadcast_to(distance / CROPW, dist_row.shape[1:])
    swap_g = remote(own_g, other_g, swap_send, swap_recv, 1, sibling)
    row_copies = [
        remote(dist_row.at[3], dist_row.at[step - 1], dist_send, dist_recv, step - 1, peer(0, step)) for step in (1, 2, 3)
    ]
    swap_g.wait_recv()
    swap_h.wait_recv()

    mixes = (
        lambda g: [g[0] + g[1] + g[2]],
        lambda g: [g[0] + g[1], g[2]],
        lambda g: g,
    )
    split = [[ref[f * cols : (f + 1) * cols, :].astype(F32) for f in range(frames)] for ref in (own_g, other_g)]
    for p in range(3):
        both = jnp.concatenate(mixes[p](split[0]) + mixes[p](split[1]), axis=0)
        rhs[p, : both.shape[0], :] = jnp.concatenate(
            [shift_rows(both, -1, cols), both, shift_rows(both, 1, cols)], axis=1
        ).astype(BF16)

    quarter_rows = quarter.shape[1]
    half_rows = quarter_rows // 2
    piece = quarter_rows // 4
    chunk_rows = 4 * quarter_rows
    own_half = pl.ds(pl.multiple_of(core * half, half), half)
    sent = {}

    def chunk_at(b, q, h, count=1):
        return pl.ds(pl.multiple_of(b * chunk_rows + lax.rem(q + 4, 4) * quarter_rows + h * half_rows, 16), half_rows * count)

    def out_rows(p, b, q, h, count=1):
        return out_ref.at[core, p, chunk_at(b, q, h, count)]

    def go(c, kind, src, dst, to):
        sent[c, kind] = remote(src, dst, send, recv, c * 27 + kind, to)

    def make(b):
        for p in range(3):
            c, m, depth = p * 3 + b, place[p], (p + 1) * cols
            lhs = jnp.concatenate([hidden_t[b, own_half, :depth], other_h[b, :, :depth]], axis=1)
            for e in range(3):
                base = b * chunk_rows + e * half
                part[p, base : base + half, :] = dot(
                    lhs, rhs[p, : 2 * depth, e * outputs : (e + 1) * outputs]
                ).astype(BF16)
            go(c, 0, part.at[p, chunk_at(b, m + 2, 0)], left1.at[c], peer(p, 1))
            go(c, 1, part.at[p, chunk_at(b, m + 2, 1)], right1.at[c], peer(p, 3))
            go(c, 2, part.at[p, chunk_at(b, m + 1, 1)], got.at[c, 0, pl.ds(half_rows, half_rows)], peer(p, 1))
            go(c, 3, part.at[p, chunk_at(b, m - 1, 0)], got.at[c, 1, pl.ds(0, half_rows)], peer(p, 3))

    def ring(b):
        for p in range(3):
            c, m = p * 3 + b, place[p]
            for way, arrived, q, step in ((0, left1, m + 1, 1), (1, right1, m - 1, 3)):
                sent[c, way].wait_recv()
                comb[c, way] = (part[p, chunk_at(b, q, way), :].astype(F32) + arrived[c].astype(F32)).astype(BF16)
                go(c, 4 + way, comb.at[c, way], got.at[c, way, pl.ds(way * half_rows, half_rows)], peer(p, step))

    def direct(b):
        for p in range(3):
            c, axis = p * 3 + b, (p + 1) % 3
            for kind in (2, 3, 4, 5):
                sent[c, kind].wait_recv()
            mine_rows = part[p, chunk_at(b, place[p], 0, 2), :].astype(F32)
            red1[c] = (mine_rows + got[c, 0].astype(F32) + got[c, 1].astype(F32)).astype(BF16)
            for step in (1, 2, 3):
                to = lax.rem(place[axis] + step, 4)
                go(c, 5 + step, red1.at[c, pl.ds(pl.multiple_of(to * piece, 16), piece)], got2.at[c, step - 1], peer(axis, step))

    def to_all(b):
        for p in range(3):
            c, axis, here = p * 3 + b, (p + 2) % 3, place[(p + 1) % 3]
            for step in (1, 2, 3):
                sent[c, 5 + step].wait_recv()
            added = red1[c, pl.ds(pl.multiple_of(here * piece, 16), piece), :].astype(F32)
            for i in range(3):
                added = added + got2[c, i].astype(F32)
            got3[c, place[axis]] = added.astype(BF16)
            for step in (1, 2, 3):
                slot = got3.at[c, place[axis]]
                go(c, 8 + step, slot, slot, peer(axis, step))

    def back(b):
        for p in range(3):
            c, axis = p * 3 + b, (p + 1) % 3
            for step in (1, 2, 3):
                sent[c, 8 + step].wait_recv()
            whole = got3[c, 0].astype(F32)
            for i in range(1, 4):
                whole = whole + got3[c, i].astype(F32)
            rows = pl.ds(pl.multiple_of(place[axis] * piece, 16), piece)
            quarter[c, rows, :] = whole.astype(BF16)
            for step in (1, 2, 3):
                slot = quarter.at[c, rows]
                go(c, 11 + step, slot, slot, peer(axis, step))

    stored = []

    def spread_out(b):
        for p in range(3):
            c, m = p * 3 + b, place[p]
            for step in (1, 2, 3):
                sent[c, 11 + step].wait_recv()
            for kind, h, step in ((0, 0, 1), (1, 1, 3), (2, 1, 1), (3, 0, 3)):
                go(c, 15 + kind, quarter.at[c, pl.ds(h * half_rows, half_rows)], out_rows(p, b, m, h), peer(p, step))
            go(c, 21, quarter.at[c], out_rows(p, b, m, 0, 2), sibling)
            store = pltpu.make_async_copy(quarter.at[c], out_rows(p, b, m, 0, 2), local.at[2 + c])
            store.start()
            stored.append(store)

    def forward(b):
        for p in range(3):
            c, m = p * 3 + b, place[p]
            for kind, q, step in ((0, m - 1, 1), (1, m + 1, 3)):
                sent[c, 15 + kind].wait_recv()
                go(c, 19 + kind, out_rows(p, b, q, kind), out_rows(p, b, q, kind), peer(p, step))

    def across(b):
        for p in range(3):
            c, m = p * 3 + b, place[p]
            for kind, q in ((2, m - 1), (3, m + 1)):
                sent[c, 15 + kind].wait_recv()
                go(c, 20 + kind, out_rows(p, b, q, 0, 2), out_rows(p, b, q, 0, 2), sibling)

    def across_last(b):
        for p in range(3):
            c, m = p * 3 + b, place[p]
            for h in range(2):
                sent[c, 19 + h].wait_recv()
                go(c, 24 + h, out_rows(p, b, m + 2, h), out_rows(p, b, m + 2, h), sibling)

    make(0)
    make(1)
    ring(0)
    make(2)

    for copy in row_copies:
        copy.wait_recv()
    dist_pair[0] = dist_row[0] + dist_row[1] + dist_row[2] + dist_row[3]
    pair = remote(dist_pair.at[0], dist_pair.at[1], dist_send, dist_recv, 3, peer(2, 2))

    ring(1)
    direct(0)
    ring(2)
    direct(1)
    to_all(0)
    direct(2)
    back(0)
    to_all(1)
    spread_out(0)
    back(1)
    to_all(2)
    forward(0)
    spread_out(1)
    back(2)
    across(0)
    forward(1)
    spread_out(2)
    across_last(0)
    across(1)
    forward(2)
    across_last(1)
    across(2)
    across_last(2)

    pair.wait()
    crops, scored = dist_pair.shape[2], dist_out.shape[1]
    pick = lax.broadcasted_iota(jnp.int32, (crops, scored), 0) == (
        mine * scored + lax.broadcasted_iota(jnp.int32, (crops, scored), 1)
    )
    dist_out[...] = jnp.dot(
        dist_pair[0] + dist_pair[1], pick.astype(F32), precision=lax.Precision.HIGHEST, preferred_element_type=F32
    )[0:1]
    for (c, kind), copy in sent.items():
        if kind >= 21:
            copy.wait_recv()
        copy.wait_send()
    for copy in stored:
        copy.wait()
    for copy in told + list(links.values()) + row_copies + [swap_g, swap_h]:
        copy.wait_send()


def widen(half_ref, out_ref):
    half = half_ref.shape[2]
    for i in range(half_ref.shape[1]):
        for h in range(2):
            out_ref[i, pl.ds(h * half, half), :] = half_ref[h, i].astype(F32)


def on_device(
    features, target, gn_gain, attn_query, attn_key, attn_value, attn_out, conv_weight, conv_bias,
    percept, lpips_weight, crop_owner, crop_frame, crop_col,
):
    tiles = lax.axis_size("tile")
    frames, rows_dev, cols, width = features.shape[1:]
    outputs = conv_weight.shape[-1]
    cells = frames * rows_dev * cols
    taps = 27
    half = width // 2
    part_rows = taps // 3 * half
    quarter = part_rows // 12
    crops = crop_col.shape[1]
    vmem = pl.BlockSpec(memory_space=pltpu.VMEM)
    hbm = pl.BlockSpec(memory_space=pl.ANY)
    sems = lambda count: pltpu.SemaphoreType.DMA((count,))
    decoded, summed, distances = pl.pallas_call(
        functools.partial(decoder_window, tiles, frames, cols),
        in_specs=[hbm] + [vmem] * 12 + [hbm],
        out_specs=[vmem, hbm, vmem],
        out_shape=[
            jax.ShapeDtypeStruct((cells, outputs), BF16),
            jax.ShapeDtypeStruct((2, 3, part_rows, outputs), BF16),
            jax.ShapeDtypeStruct((1, crops // tiles), F32),
        ],
        scratch_shapes=[
            pltpu.VMEM((taps, width, outputs), BF16),
            pltpu.VMEM((tiles, cells, width), BF16),
            pltpu.VMEM((tiles * cells, width), BF16),
            pltpu.VMEM((tiles, 8, width), F32),
            pltpu.VMEM((3 * cells, width), BF16),
            pltpu.VMEM((3 * cells, width), F32),
            pltpu.VMEM((3 * cells, 128), F32),
            pltpu.VMEM((3 * cells, 128), F32),
            pltpu.VMEM((3, cells, width), BF16),
            pltpu.VMEM((3, width, cells), BF16),
            pltpu.VMEM((3, half, cells), BF16),
            pltpu.VMEM((cells, outputs), BF16),
            pltpu.VMEM((cells, outputs), BF16),
            pltpu.VMEM((3, 2 * cells, 3 * outputs), BF16),
            pltpu.VMEM((3, part_rows, outputs), BF16),
            pltpu.VMEM((9, quarter // 2, outputs), BF16),
            pltpu.VMEM((9, quarter // 2, outputs), BF16),
            pltpu.VMEM((9, 2, quarter // 2, outputs), BF16),
            pltpu.VMEM((9, 2, quarter, outputs), BF16),
            pltpu.VMEM((9, quarter, outputs), BF16),
            pltpu.VMEM((9, 3, quarter // 4, outputs), BF16),
            pltpu.VMEM((9, 4, quarter // 4, outputs), BF16),
            pltpu.VMEM((9, quarter, outputs), BF16),
            pltpu.VMEM((4, 8, crops), F32),
            pltpu.VMEM((2, 8, crops), F32),
            sems(14), sems(14), sems(tiles - 1), sems(tiles - 1), sems(2), sems(2), sems(4), sems(4),
            sems(9 * 27), sems(9 * 27), sems(11),
        ],
        compiler_params=pltpu.CompilerParams(
            collective_id=1, has_side_effects=True, vmem_limit_bytes=60 * 1024 * 1024
        ),
        cost_estimate=pl.CostEstimate(flops=14_000_000_000, bytes_accessed=24_000_000, transcendentals=4_000_000),
        name="decoder_window",
    )(
        features.reshape(cells, width), target.reshape(cells, outputs), gn_gain[None, :],
        attn_query, attn_key, attn_value, attn_out, conv_bias[None, :], percept, lpips_weight[None, :],
        crop_owner.reshape(1, -1), crop_frame, crop_col, conv_weight.reshape(taps, width, outputs),
    )
    conv_total = pl.pallas_call(
        widen,
        grid=(taps // 3,),
        in_specs=[pl.BlockSpec((2, 3, half, outputs), lambda i: (0, i, 0, 0))],
        out_specs=pl.BlockSpec((3, width, outputs), lambda i: (i, 0, 0)),
        out_shape=jax.ShapeDtypeStruct((taps, width, outputs), F32),
        name="widen",
    )(summed.reshape(2, taps, half, outputs)).reshape(conv_weight.shape)
    return (decoded.reshape(1, frames, rows_dev, cols, outputs), conv_total, distances)


def solution(mesh):
    return jax.shard_map(
        on_device,
        mesh=mesh,
        in_specs=(
            P("clip", None, "tile", None, None),
            P("clip", None, "tile", None, None),
            P(), P(), P(), P(), P(), P(), P(), P(), P(),
            P("clip", None, None),
            P("clip", None),
            P("clip", None),
        ),
        out_specs=(P("clip", None, "tile", None, None), P(), P("clip", "tile")),
        check_vma=False,
    )
```

time: 651 us -> 110 us (0.17)
  waiting for transfers between devices: 318 us -> 0 us
  local copies, waits for them, and re-layouts: 125 us -> 1.2 us
  Pallas kernels: 0 us -> 107 us
  matrix products: 66.8 us -> 0 us
  loops' own time: 53.8 us -> 0 us
  other arithmetic: 28.5 us -> 0 us
  blocking collectives: 22.1 us -> 0 us
  starting transfers between devices: 17 us -> 0 us
  between operations: 14.7 us -> 0.66 us
    psum x1 -> x0, waiting for transfers between devices: 172 us -> none  [on_device(): conv_total = lax.psum(local_grad, ('clip', 'tile'))]
    all_gather x2 -> x0, waiting for transfers between devices: 113 us -> none  [the longest x1 58.6 us: on_device(): lax.all_gather(keys_local, 'tile', axis=0, tiled=True)]
    pallas_call x0 -> x2, Pallas kernels: none -> 107 us  [the longest x1 97.3 us: on_device(): pl.pallas_call(functools.partial(decoder_window, tiles, frames, cols), in...]
    dot_general x61 -> x0, matrix products: 66.8 us -> none  [the longest x27 38.9 us: conv_forward(): jnp.dot(tap, conv_weight[offset_t, offset_y, offset_x], preferred_element...]
    another operation x1 -> x0, loops' own time: 53.8 us -> none  [on_device(): lax.fori_loop(0, tiles * CAP, add_slot, jnp.zeros((frames, rows_dev, cols...]
    slice x26 -> x0, local copies, waits for them, and re-layouts: 50.3 us -> none  [conv_forward(): padded[offset_t:offset_t + frames, offset_y:offset_y + rows, offset_x:off...]
    all_to_all x2 -> x0, waiting for transfers between devices: 24.3 us -> none  [the longest x1 15.3 us: on_device(): lax.all_to_all(packed, 'tile', split_axis=0, concat_axis=0, tiled=True)]
    dynamic_update_slice x16 -> x0, local copies, waits for them, and re-layouts: 24.3 us -> none  [add_slot(): return lax.dynamic_update_slice(grad_map, current + update, start)]
  transfers between devices with their start and end apart: 7 -> 0, of which waited for: 7 -> 0; matrix products, arithmetic and copies ran while one was open for 3% -> 0% of each run, Pallas kernels for 0% -> 0%
where the time goes in v2:
time: 110 us; the launch traced here: 109 us
  Pallas kernels  107 us (97%)
  local copies, waits for them, and re-layouts  1.2 us (1%)
    pallas_call x1, Pallas kernels, on_device(): pl.pallas_call(functools.partial(decoder_window, tiles, frames, cols), in...  97.3 us
    pallas_call x1, Pallas kernels, on_device(): pl.pallas_call(widen, grid=(taps // 3,), in_specs=[pl.BlockSpec((2, 3, ha...  10 us

profile of v2, /device:TPU:1, one launch (start us, length us, event | category | flops | bytes accessed | tf_op | source)
XLA Modules:
  0.0 109.2 jit_solution(11966657766712815139)
XLA Ops:
  0.6 97.3 %decoder_window.1 = (bf16[384,256]{1,0:T(8,128)(2,1)}, bf16[2,3,2304,256]{3,2,1,0:T(8,128)(2,1)}, f32[1,8]{1,0:T(1,128)}) custom-call(bf16[384,512]{1,0:T(8,128)(2,1)} %bitcast.16, bf16[384,256]{1,0:T(8,128)(2,1)} %bitcast.17, f32[1,512]{1,0:T(1,128)} %bitcast.18, bf16[512,512]{1,0:T(8,128)(2,1)} %wq_ref.1, bf16[512,512]{1,0:T(8,128)(2,1)} %wk_ref.1, ...), custom_call_target="tpu_custom_call" | custom-call | flops 14000000000 | bytes 24000000 | tf_op jit(solution)/shard_map/decoder_window/pallas_call | solution.py:494
  97.9 0.0 copy-start
  98.0 0.0 copy-start.1
  98.0 10.0 %widen.1 = f32[27,512,256]{2,1,0:T(8,128)} custom-call(bf16[2,27,256,256]{3,2,1,0:T(8,128)(2,1)} %bitcast.13), custom_call_target="tpu_custom_call" | custom-call | tf_op jit(solution)/shard_map/widen/pallas_call | solution.py:542
  108.0 0.0 copy-done
  108.0 0.7 copy.20
  108.7 0.0 copy-done.1
  108.7 0.5 copy.21
Async XLA Ops:
  97.9 10.0 %copy-start = (bf16[384,256]{1,0:T(8,128)(2,1)S(1)}, bf16[384,256]{1,0:T(8,128)(2,1)}, u32[]{:S(2)}) copy-start(bf16[384,256]{1,0:T(8,128)(2,1)} %get-tuple-element.6) | copy-start | bytes 589828
  98.0 10.7 %copy-start.1 = (f32[1,8]{1,0:T(1,128)S(1)}, f32[1,8]{1,0:T(1,128)}, u32[]{:S(2)}) copy-start(f32[1,8]{1,0:T(1,128)} %get-tuple-element.17) | copy-start | bytes 100

commit v3 on v2

--- a/solution.py
+++ b/solution.py
@@ -70,7 +70,7 @@
     decoded_ref, out_ref, dist_out,
     weight, feats, normed, stats, qs, acc, peak, total, hidden, hidden_t, other_h, own_g, other_g, rhs,
     part, left1, right1, comb, got, red1, got2, got3, quarter, dist_row, dist_pair,
-    gather_send, gather_recv, stat_send, stat_recv, swap_send, swap_recv, dist_send, dist_recv, send, recv, local,
+    once, gather_recv, recv, local,
 ):
     place, core = chip_place()
     clip = lax.axis_index("clip")
@@ -88,13 +88,16 @@
     def peer(axis, step):
         return device_at(on_axis(place, axis, place[axis] + step), core)
 
-    def remote(src, dst, sems, rsems, index, target):
+    def remote(src, dst, sent_sem, got_sem, target):
         copy = pltpu.make_async_remote_copy(
-            src_ref=src, dst_ref=dst, send_sem=sems.at[index], recv_sem=rsems.at[index],
+            src_ref=src, dst_ref=dst, send_sem=sent_sem, recv_sem=got_sem,
             device_id=target, device_id_type=pl.DeviceIdType.MESH,
         )
         copy.start()
         return copy
+
+    def take(rows, sem):
+        pltpu.make_async_copy(rows, rows, sem).wait()
 
     own, left, right, opposite = (tile_at(step, 0) for step in (0, -1, 1, 2))
     partner, left2, right2, opposite2 = (tile_at(step, 1) for step in (0, -1, 1, 2))
@@ -119,13 +122,12 @@
         axis=0,
     )
     pl.semaphore_wait(barrier, len(peers))
-    told = [
-        remote(stats.at[own], stats.at[own], stat_send, stat_recv, step, peers[step]) for step in range(tiles - 1)
-    ]
+    for step in range(tiles - 1):
+        remote(stats.at[own], stats.at[own], once.at[0], once.at[1], peers[step])
 
     def pass_on(index, unit, h, to):
         rows = feats.at[unit, pl.ds(h * cut, cut)]
-        return remote(rows, rows, gather_send, gather_recv, index, (clip, to))
+        return remote(rows, rows, once.at[2], gather_recv.at[index], (clip, to))
 
     links = {}
     links["z0"] = pass_on(0, own, 0, partner)
@@ -137,8 +139,7 @@
 
     lane = lax.broadcasted_iota(jnp.int32, (width, width), 0) // (width // GROUPS)
     same = (lane == lax.broadcasted_iota(jnp.int32, (width, width), 1) // (width // GROUPS)).astype(BF16)
-    for copy in told:
-        copy.wait_recv()
+    take(stats.at[pl.ds(0, tiles - 1)], once.at[1])
     sums = stats[0]
     for i in range(1, tiles):
         sums = sums + stats[i]
@@ -203,6 +204,7 @@
     links["o0"].wait_recv()
     links["o1"].wait_recv()
     normalize(4, opposite)
+    attend((0, 2), (4, 5), False)
     links["l2"].wait_recv()
     links["p0"] = pass_on(12, left2, 0, right)
     links["r3"].wait_recv()
@@ -212,12 +214,12 @@
     normalize(5, far)
     normalize(6, near)
     make_queries(2, 5)
-    attend((2, 3), (0, 4), True)
-    attend((0, 3), (4, 6), False)
+    attend((2, 3), (0, 5), True)
+    attend((0, 3), (5, 7), False)
     links["p0"].wait_recv()
     links["p1"].wait_recv()
     normalize(7, opposite2)
-    attend((0, 3), (6, 8), False)
+    attend((0, 3), (7, 8), False)
 
     def choose(i, values):
         chosen = values[0]
@@ -241,7 +243,7 @@
 
     lax.fori_loop(0, 3, finish, 0)
     swap_h = remote(
-        hidden_t.at[:, pl.ds(pl.multiple_of((1 - core) * half, half), half)], other_h, swap_send, swap_recv, 0, sibling
+        hidden_t.at[:, pl.ds(pl.multiple_of((1 - core) * half, half), half)], other_h, once.at[3], once.at[4], sibling
     )
     fetch.wait()
 
@@ -286,31 +288,34 @@
         distance = distance + jnp.sum(cover * apart[rows], axis=0, keepdims=True)
         own_g[rows, :] = (pull[rows] * jnp.sum(cover, axis=1, keepdims=True)).astype(BF16)
     dist_row[3] = jnp.broadcast_to(distance / CROPW, dist_row.shape[1:])
-    swap_g = remote(own_g, other_g, swap_send, swap_recv, 1, sibling)
-    row_copies = [
-        remote(dist_row.at[3], dist_row.at[step - 1], dist_send, dist_recv, step - 1, peer(0, step)) for step in (1, 2, 3)
-    ]
-    swap_g.wait_recv()
-    swap_h.wait_recv()
+    swap_g = remote(own_g, other_g, once.at[5], once.at[6], sibling)
+    for step in (1, 2, 3):
+        remote(dist_row.at[3], dist_row.at[step - 1], once.at[7], once.at[8], peer(0, step))
 
     mixes = (
         lambda g: [g[0] + g[1] + g[2]],
         lambda g: [g[0] + g[1], g[2]],
         lambda g: g,
     )
-    split = [[ref[f * cols : (f + 1) * cols, :].astype(F32) for f in range(frames)] for ref in (own_g, other_g)]
-    for p in range(3):
-        both = jnp.concatenate(mixes[p](split[0]) + mixes[p](split[1]), axis=0)
-        rhs[p, : both.shape[0], :] = jnp.concatenate(
-            [shift_rows(both, -1, cols), both, shift_rows(both, 1, cols)], axis=1
-        ).astype(BF16)
+
+    def line_up(ref, place_in):
+        g = [ref[f * cols : (f + 1) * cols, :].astype(F32) for f in range(frames)]
+        for p in range(3):
+            mixed = jnp.concatenate(mixes[p](g), axis=0)
+            depth = mixed.shape[0]
+            for e, moved in enumerate((shift_rows(mixed, -1, cols), mixed, shift_rows(mixed, 1, cols))):
+                rhs[p, place_in * depth : (place_in + 1) * depth, e * outputs : (e + 1) * outputs] = moved.astype(BF16)
+
+    line_up(own_g, 0)
+    swap_g.wait_recv()
+    line_up(other_g, 1)
+    swap_h.wait_recv()
 
     quarter_rows = quarter.shape[1]
     half_rows = quarter_rows // 2
     piece = quarter_rows // 4
     chunk_rows = 4 * quarter_rows
     own_half = pl.ds(pl.multiple_of(core * half, half), half)
-    sent = {}
 
     def chunk_at(b, q, h, count=1):
         return pl.ds(pl.multiple_of(b * chunk_rows + lax.rem(q + 4, 4) * quarter_rows + h * half_rows, 16), half_rows * count)
@@ -318,8 +323,11 @@
     def out_rows(p, b, q, h, count=1):
         return out_ref.at[core, p, chunk_at(b, q, h, count)]
 
-    def go(c, kind, src, dst, to):
-        sent[c, kind] = remote(src, dst, send, recv, c * 27 + kind, to)
+    def go(c, stage, src, dst, to):
+        remote(src, dst, once.at[9 if stage < 5 else 10], recv.at[c, stage], to)
+
+    def across_to(src, dst):
+        remote(src, dst, once.at[10], once.at[11], sibling)
 
     def make(b):
         for p in range(3):
@@ -331,47 +339,44 @@
                     lhs, rhs[p, : 2 * depth, e * outputs : (e + 1) * outputs]
                 ).astype(BF16)
             go(c, 0, part.at[p, chunk_at(b, m + 2, 0)], left1.at[c], peer(p, 1))
-            go(c, 1, part.at[p, chunk_at(b, m + 2, 1)], right1.at[c], peer(p, 3))
-            go(c, 2, part.at[p, chunk_at(b, m + 1, 1)], got.at[c, 0, pl.ds(half_rows, half_rows)], peer(p, 1))
-            go(c, 3, part.at[p, chunk_at(b, m - 1, 0)], got.at[c, 1, pl.ds(0, half_rows)], peer(p, 3))
+            go(c, 0, part.at[p, chunk_at(b, m + 2, 1)], right1.at[c], peer(p, 3))
+            go(c, 1, part.at[p, chunk_at(b, m + 1, 1)], got.at[c, 0, pl.ds(half_rows, half_rows)], peer(p, 1))
+            go(c, 1, part.at[p, chunk_at(b, m - 1, 0)], got.at[c, 1, pl.ds(0, half_rows)], peer(p, 3))
 
     def ring(b):
         for p in range(3):
             c, m = p * 3 + b, place[p]
+            take(comb.at[c], recv.at[c, 0])
             for way, arrived, q, step in ((0, left1, m + 1, 1), (1, right1, m - 1, 3)):
-                sent[c, way].wait_recv()
                 comb[c, way] = (part[p, chunk_at(b, q, way), :].astype(F32) + arrived[c].astype(F32)).astype(BF16)
-                go(c, 4 + way, comb.at[c, way], got.at[c, way, pl.ds(way * half_rows, half_rows)], peer(p, step))
+                go(c, 1, comb.at[c, way], got.at[c, way, pl.ds(way * half_rows, half_rows)], peer(p, step))
 
     def direct(b):
         for p in range(3):
             c, axis = p * 3 + b, (p + 1) % 3
-            for kind in (2, 3, 4, 5):
-                sent[c, kind].wait_recv()
+            take(got.at[c], recv.at[c, 1])
             mine_rows = part[p, chunk_at(b, place[p], 0, 2), :].astype(F32)
             red1[c] = (mine_rows + got[c, 0].astype(F32) + got[c, 1].astype(F32)).astype(BF16)
             for step in (1, 2, 3):
                 to = lax.rem(place[axis] + step, 4)
-                go(c, 5 + step, red1.at[c, pl.ds(pl.multiple_of(to * piece, 16), piece)], got2.at[c, step - 1], peer(axis, step))
+                go(c, 2, red1.at[c, pl.ds(pl.multiple_of(to * piece, 16), piece)], got2.at[c, step - 1], peer(axis, step))
 
     def to_all(b):
         for p in range(3):
             c, axis, here = p * 3 + b, (p + 2) % 3, place[(p + 1) % 3]
-            for step in (1, 2, 3):
-                sent[c, 5 + step].wait_recv()
+            take(got2.at[c], recv.at[c, 2])
             added = red1[c, pl.ds(pl.multiple_of(here * piece, 16), piece), :].astype(F32)
             for i in range(3):
                 added = added + got2[c, i].astype(F32)
             got3[c, place[axis]] = added.astype(BF16)
             for step in (1, 2, 3):
                 slot = got3.at[c, place[axis]]
-                go(c, 8 + step, slot, slot, peer(axis, step))
+                go(c, 3, slot, slot, peer(axis, step))
 
     def back(b):
         for p in range(3):
             c, axis = p * 3 + b, (p + 1) % 3
-            for step in (1, 2, 3):
-                sent[c, 8 + step].wait_recv()
+            take(got2.at[c], recv.at[c, 3])
             whole = got3[c, 0].astype(F32)
             for i in range(1, 4):
                 whole = whole + got3[c, i].astype(F32)
@@ -379,76 +384,51 @@
             quarter[c, rows, :] = whole.astype(BF16)
             for step in (1, 2, 3):
                 slot = quarter.at[c, rows]
-                go(c, 11 + step, slot, slot, peer(axis, step))
-
-    stored = []
+                go(c, 4, slot, slot, peer(axis, step))
 
     def spread_out(b):
         for p in range(3):
             c, m = p * 3 + b, place[p]
-            for step in (1, 2, 3):
-                sent[c, 11 + step].wait_recv()
-            for kind, h, step in ((0, 0, 1), (1, 1, 3), (2, 1, 1), (3, 0, 3)):
-                go(c, 15 + kind, quarter.at[c, pl.ds(h * half_rows, half_rows)], out_rows(p, b, m, h), peer(p, step))
-            go(c, 21, quarter.at[c], out_rows(p, b, m, 0, 2), sibling)
-            store = pltpu.make_async_copy(quarter.at[c], out_rows(p, b, m, 0, 2), local.at[2 + c])
-            store.start()
-            stored.append(store)
+            take(got2.at[c], recv.at[c, 4])
+            for stage, h, step in ((5, 0, 1), (5, 1, 3), (6, 1, 1), (6, 0, 3)):
+                go(c, stage, quarter.at[c, pl.ds(h * half_rows, half_rows)], out_rows(p, b, m, h), peer(p, step))
+            across_to(quarter.at[c], out_rows(p, b, m, 0, 2))
+            pltpu.make_async_copy(quarter.at[c], out_rows(p, b, m, 0, 2), local.at[2]).start()
 
     def forward(b):
         for p in range(3):
             c, m = p * 3 + b, place[p]
-            for kind, q, step in ((0, m - 1, 1), (1, m + 1, 3)):
-                sent[c, 15 + kind].wait_recv()
-                go(c, 19 + kind, out_rows(p, b, q, kind), out_rows(p, b, q, kind), peer(p, step))
+            take(quarter.at[c], recv.at[c, 5])
+            for h, q, step in ((0, m - 1, 1), (1, m + 1, 3)):
+                go(c, 7, out_rows(p, b, q, h), out_rows(p, b, q, h), peer(p, step))
 
     def across(b):
         for p in range(3):
             c, m = p * 3 + b, place[p]
-            for kind, q in ((2, m - 1), (3, m + 1)):
-                sent[c, 15 + kind].wait_recv()
-                go(c, 20 + kind, out_rows(p, b, q, 0, 2), out_rows(p, b, q, 0, 2), sibling)
+            take(quarter.at[c], recv.at[c, 6])
+            for q in (m - 1, m + 1):
+                across_to(out_rows(p, b, q, 0, 2), out_rows(p, b, q, 0, 2))
 
     def across_last(b):
         for p in range(3):
             c, m = p * 3 + b, place[p]
-            for h in range(2):
-                sent[c, 19 + h].wait_recv()
-                go(c, 24 + h, out_rows(p, b, m + 2, h), out_rows(p, b, m + 2, h), sibling)
+            take(quarter.at[c], recv.at[c, 7])
+            across_to(out_rows(p, b, m + 2, 0, 2), out_rows(p, b, m + 2, 0, 2))
 
     make(0)
     make(1)
     ring(0)
     make(2)
-
-    for copy in row_copies:
-        copy.wait_recv()
+    ring(1)
+
+    take(dist_row.at[pl.ds(0, 3)], once.at[8])
     dist_pair[0] = dist_row[0] + dist_row[1] + dist_row[2] + dist_row[3]
-    pair = remote(dist_pair.at[0], dist_pair.at[1], dist_send, dist_recv, 3, peer(2, 2))
-
-    ring(1)
-    direct(0)
+    pair = remote(dist_pair.at[0], dist_pair.at[1], once.at[12], once.at[13], peer(2, 2))
+
     ring(2)
-    direct(1)
-    to_all(0)
-    direct(2)
-    back(0)
-    to_all(1)
-    spread_out(0)
-    back(1)
-    to_all(2)
-    forward(0)
-    spread_out(1)
-    back(2)
-    across(0)
-    forward(1)
-    spread_out(2)
-    across_last(0)
-    across(1)
-    forward(2)
-    across_last(1)
-    across(2)
-    across_last(2)
+    for stage in (direct, to_all, back, spread_out, forward, across, across_last):
+        for b in range(3):
+            stage(b)
 
     pair.wait()
     crops, scored = dist_pair.shape[2], dist_out.shape[1]
@@ -458,14 +438,15 @@
     dist_out[...] = jnp.dot(
         dist_pair[0] + dist_pair[1], pick.astype(F32), precision=lax.Precision.HIGHEST, preferred_element_type=F32
     )[0:1]
-    for (c, kind), copy in sent.items():
-        if kind >= 21:
-            copy.wait_recv()
-        copy.wait_send()
-    for copy in stored:
-        copy.wait()
-    for copy in told + list(links.values()) + row_copies + [swap_g, swap_h]:
-        copy.wait_send()
+    take(out_ref.at[1 - core], once.at[11])
+    take(quarter, local.at[2])
+    take(stats.at[pl.ds(0, tiles - 1)], once.at[0])
+    take(feats.at[pl.ds(0, 7)], once.at[2])
+    take(dist_row.at[pl.ds(0, 3)], once.at[7])
+    take(weight.at[:, pl.ds(0, 9 * 21 * half_rows // 54)], once.at[9])
+    take(weight.at[:, pl.ds(0, 9 * 14 * half_rows // 27)], once.at[10])
+    swap_g.wait_send()
+    swap_h.wait_send()
 
 
 def widen(half_ref, out_ref):
@@ -526,8 +507,7 @@
             pltpu.VMEM((9, quarter, outputs), BF16),
             pltpu.VMEM((4, 8, crops), F32),
             pltpu.VMEM((2, 8, crops), F32),
-            sems(14), sems(14), sems(tiles - 1), sems(tiles - 1), sems(2), sems(2), sems(4), sems(4),
-            sems(9 * 27), sems(9 * 27), sems(11),
+            sems(14), sems(14), pltpu.SemaphoreType.DMA((9, 8)), sems(3),
         ],
         compiler_params=pltpu.CompilerParams(
             collective_id=1, has_side_effects=True, vmem_limit_bytes=60 * 1024 * 1024

time: 110 us -> 101 us (0.918)
  Pallas kernels: 107 us -> 98.4 us
    pallas_call x1, Pallas kernels: 97.3 us -> 88.3 us  [on_device(): pl.pallas_call(functools.partial(decoder_window, tiles, frames, cols), in...]
where the time goes in v3:
time: 101 us; the launch traced here: 100 us
  Pallas kernels  98.4 us (97%)
  local copies, waits for them, and re-layouts  1.2 us (1%)
    pallas_call x1, Pallas kernels, on_device(): pl.pallas_call(functools.partial(decoder_window, tiles, frames, cols), in...  88.3 us
    pallas_call x1, Pallas kernels, on_device(): pl.pallas_call(widen, grid=(taps // 3,), in_specs=[pl.BlockSpec((2, 3, ha...  10 us

profile of v3, /device:TPU:1, one launch (start us, length us, event | category | flops | bytes accessed | tf_op | source)
XLA Modules:
  0.0 100.2 jit_solution(8323055844569791368)
XLA Ops:
  0.6 88.3 %decoder_window.1 = (bf16[384,256]{1,0:T(8,128)(2,1)}, bf16[2,3,2304,256]{3,2,1,0:T(8,128)(2,1)}, f32[1,8]{1,0:T(1,128)}) custom-call(bf16[384,512]{1,0:T(8,128)(2,1)} %bitcast.16, bf16[384,256]{1,0:T(8,128)(2,1)} %bitcast.17, f32[1,512]{1,0:T(1,128)} %bitcast.18, bf16[512,512]{1,0:T(8,128)(2,1)} %wq_ref.1, bf16[512,512]{1,0:T(8,128)(2,1)} %wk_ref.1, ...), custom_call_target="tpu_custom_call" | custom-call | flops 14000000000 | bytes 24000000 | tf_op jit(solution)/shard_map/decoder_window/pallas_call | solution.py:475
  89.0 0.0 copy-start
  89.0 0.0 copy-start.1
  89.0 10.0 %widen.1 = f32[27,512,256]{2,1,0:T(8,128)} custom-call(bf16[2,27,256,256]{3,2,1,0:T(8,128)(2,1)} %bitcast.13), custom_call_target="tpu_custom_call" | custom-call | tf_op jit(solution)/shard_map/widen/pallas_call | solution.py:522
  99.0 0.0 copy-done
  99.0 0.7 copy.20
  99.7 0.0 copy-done.1
  99.7 0.5 copy.21
Async XLA Ops:
  89.0 10.0 %copy-start = (bf16[384,256]{1,0:T(8,128)(2,1)S(1)}, bf16[384,256]{1,0:T(8,128)(2,1)}, u32[]{:S(2)}) copy-start(bf16[384,256]{1,0:T(8,128)(2,1)} %get-tuple-element.6) | copy-start | bytes 589828
  89.0 10.7 %copy-start.1 = (f32[1,8]{1,0:T(1,128)S(1)}, f32[1,8]{1,0:T(1,128)}, u32[]{:S(2)}) copy-start(f32[1,8]{1,0:T(1,128)} %get-tuple-element.17) | copy-start | bytes 100

commit v4 on v3

--- a/solution.py
+++ b/solution.py
@@ -65,10 +65,10 @@
 
 def decoder_window(
     tiles, frames, cols,
-    features, target_ref, gain_ref, wq_ref, wk_ref, wv_ref, wo_ref, bias_ref, percept_ref, lpips_ref,
-    owner_ref, frame_ref, col_ref, weight_hbm,
+    features, target_hbm, wq_hbm, wk_hbm, wv_hbm, wo_hbm, percept_hbm, weight_hbm,
+    gain_ref, bias_ref, lpips_ref, owner_ref, frame_ref, col_ref,
     decoded_ref, out_ref, dist_out,
-    weight, feats, normed, stats, qs, acc, peak, total, hidden, hidden_t, other_h, own_g, other_g, rhs,
+    weight, wq_ref, wk_ref, wv_ref, wo_ref, percept_ref, target_ref, feats, normed, stats, qs, acc, peak, total, hidden, hidden_t, other_h, own_g, other_g, rhs,
     part, left1, right1, comb, got, red1, got2, got3, quarter, dist_row, dist_pair,
     once, gather_recv, recv, local,
 ):
@@ -112,8 +112,26 @@
         pl.semaphore_signal(barrier, inc=1, device_id=other, device_id_type=pl.DeviceIdType.MESH)
     load = pltpu.make_async_copy(features, feats.at[own], local.at[0])
     load.start()
+    early = [
+        pltpu.make_async_copy(source, ref, local.at[3 + i])
+        for i, (source, ref) in enumerate(
+            ((wq_hbm, wq_ref), (wk_hbm, wk_ref), (wv_hbm, wv_ref), (wo_hbm, wo_ref), (percept_hbm, percept_ref), (target_hbm, target_ref))
+        )
+    ]
+    for copy in early:
+        copy.start()
     fetch = pltpu.make_async_copy(weight_hbm, weight, local.at[1])
-    fetch.start()
+
+    def pass_on(index, unit, h, to, mine_too=False):
+        rows = feats.at[unit, pl.ds(h * cut, cut)]
+        source = features.at[pl.ds(h * cut, cut)] if mine_too else rows
+        return remote(source, rows, once.at[2], gather_recv.at[index], (clip, to))
+
+    links = {}
+    pl.semaphore_wait(barrier, len(peers))
+    links["l0"] = pass_on(1, own, 0, right, True)
+    links["r1"] = pass_on(2, own, 1, left, True)
+    links["z0"] = pass_on(0, own, 0, partner, True)
 
     load.wait()
     wide = feats[own].astype(F32)
@@ -121,24 +139,22 @@
         [jnp.sum(wide, axis=0, keepdims=True), jnp.sum(wide * wide, axis=0, keepdims=True), jnp.zeros((6, width), F32)],
         axis=0,
     )
-    pl.semaphore_wait(barrier, len(peers))
     for step in range(tiles - 1):
         remote(stats.at[own], stats.at[own], once.at[0], once.at[1], peers[step])
-
-    def pass_on(index, unit, h, to):
-        rows = feats.at[unit, pl.ds(h * cut, cut)]
-        return remote(rows, rows, once.at[2], gather_recv.at[index], (clip, to))
-
-    links = {}
-    links["z0"] = pass_on(0, own, 0, partner)
-    links["l0"] = pass_on(1, own, 0, right)
-    links["r1"] = pass_on(2, own, 1, left)
-    links["z1"] = pass_on(3, own, 1, partner)
-    links["l1"] = pass_on(4, own, 1, right)
-    links["r0"] = pass_on(5, own, 0, left)
+    links["l1"] = pass_on(4, own, 1, right, True)
+    links["r0"] = pass_on(5, own, 0, left, True)
+    links["z1"] = pass_on(3, own, 1, partner, True)
+    fetch.start()
 
     lane = lax.broadcasted_iota(jnp.int32, (width, width), 0) // (width // GROUPS)
     same = (lane == lax.broadcasted_iota(jnp.int32, (width, width), 1) // (width // GROUPS)).astype(BF16)
+    links["l0"].wait_recv()
+    links["o0"] = pass_on(6, left, 0, right)
+    links["r1"].wait_recv()
+    links["o1"] = pass_on(7, right, 1, left)
+    links["z0"].wait_recv()
+    links["l2"] = pass_on(8, partner, 0, right)
+    links["r2"] = pass_on(11, partner, 0, left)
     take(stats.at[pl.ds(0, tiles - 1)], once.at[1])
     sums = stats[0]
     for i in range(1, tiles):
@@ -182,33 +198,29 @@
                 acc[here, j : j + 128] = acc[here, j : j + 128] * fade + out[:, j : j + 128]
         peak[here, :] = new
 
+    for copy in early:
+        copy.wait()
     normalize(0, own)
     make_queries(0, 0)
-    links["l0"].wait_recv()
-    links["o0"] = pass_on(6, left, 0, right)
-    links["r1"].wait_recv()
-    links["o1"] = pass_on(7, right, 1, left)
-    links["z0"].wait_recv()
-    links["l2"] = pass_on(8, partner, 0, right)
     links["z1"].wait_recv()
     links["r3"] = pass_on(9, partner, 1, left)
     links["l3"] = pass_on(10, partner, 1, right)
-    links["r2"] = pass_on(11, partner, 0, left)
     normalize(1, partner)
     make_queries(1, 1)
     links["l1"].wait_recv()
     links["r0"].wait_recv()
     normalize(2, left)
     normalize(3, right)
-    attend((0, 2), (0, 4), True)
+    attend((0, 1), (0, 4), True)
     links["o0"].wait_recv()
+    links["p0"] = pass_on(12, opposite, 0, partner)
     links["o1"].wait_recv()
+    links["p1"] = pass_on(13, opposite, 1, partner)
+    attend((1, 2), (0, 4), True)
     normalize(4, opposite)
     attend((0, 2), (4, 5), False)
     links["l2"].wait_recv()
-    links["p0"] = pass_on(12, left2, 0, right)
     links["r3"].wait_recv()
-    links["p1"] = pass_on(13, right2, 1, left)
     links["l3"].wait_recv()
     links["r2"].wait_recv()
     normalize(5, far)
@@ -231,14 +243,14 @@
         here = pl.ds(pl.multiple_of(role * cells, cells), cells)
         unit = choose(role, [own, partner, far])
         b = choose(role, [1, 2 - 2 * side, 2 * side])
-        whole = jnp.sum(total[here, :], axis=1, keepdims=True)
-        context = (acc[here, :] / whole).astype(BF16)
+        whole = 1.0 / jnp.sum(total[here, :], axis=1, keepdims=True)
+        context = (acc[here, :] * whole).astype(BF16)
         mixed = dot(context, wv_ref[...]).astype(BF16)
         row = feats[unit].astype(F32) + dot(mixed, wo_ref[...])
         inside = (mine + b >= 1) & (mine + b <= tiles)
-        row = jnp.where(inside, row, 0.0)
-        hidden[b] = row.astype(BF16)
-        hidden_t[b] = row.T.astype(BF16)
+        row = jnp.where(inside, row, 0.0).astype(BF16)
+        hidden[b] = row
+        hidden_t[b] = row.T
         return 0
 
     lax.fori_loop(0, 3, finish, 0)
@@ -449,11 +461,23 @@
     swap_h.wait_send()
 
 
-def widen(half_ref, out_ref):
-    half = half_ref.shape[2]
-    for i in range(half_ref.shape[1]):
-        for h in range(2):
-            out_ref[i, pl.ds(h * half, half), :] = half_ref[h, i].astype(F32)
+def widen(halves, out_hbm, near, wide, in_sems, out_sems):
+    taps, half = halves.shape[1:3]
+    steps = in_sems.shape[0]
+    count = taps // steps
+    pieces = [pl.ds(i * count, count) for i in range(steps)]
+    loads = [pltpu.make_async_copy(halves.at[:, rows], near.at[:, rows], in_sems.at[i]) for i, rows in enumerate(pieces)]
+    stores = [pltpu.make_async_copy(wide.at[rows], out_hbm.at[rows], out_sems.at[i]) for i, rows in enumerate(pieces)]
+    for copy in loads:
+        copy.start()
+    for i in range(steps):
+        loads[i].wait()
+        for tap in range(i * count, (i + 1) * count):
+            for h in range(2):
+                wide[tap, h * half : (h + 1) * half, :] = near[h, tap].astype(F32)
+        stores[i].start()
+    for copy in stores:
+        copy.wait()
 
 
 def on_device(
@@ -474,7 +498,7 @@
     sems = lambda count: pltpu.SemaphoreType.DMA((count,))
     decoded, summed, distances = pl.pallas_call(
         functools.partial(decoder_window, tiles, frames, cols),
-        in_specs=[hbm] + [vmem] * 12 + [hbm],
+        in_specs=[hbm] * 8 + [vmem] * 6,
         out_specs=[vmem, hbm, vmem],
         out_shape=[
             jax.ShapeDtypeStruct((cells, outputs), BF16),
@@ -483,6 +507,12 @@
         ],
         scratch_shapes=[
             pltpu.VMEM((taps, width, outputs), BF16),
+            pltpu.VMEM((width, width), BF16),
+            pltpu.VMEM((width, width), BF16),
+            pltpu.VMEM((width, width), BF16),
+            pltpu.VMEM((width, width), BF16),
+            pltpu.VMEM((outputs, outputs), BF16),
+            pltpu.VMEM((cells, outputs), BF16),
             pltpu.VMEM((tiles, cells, width), BF16),
             pltpu.VMEM((tiles * cells, width), BF16),
             pltpu.VMEM((tiles, 8, width), F32),
@@ -507,7 +537,7 @@
             pltpu.VMEM((9, quarter, outputs), BF16),
             pltpu.VMEM((4, 8, crops), F32),
             pltpu.VMEM((2, 8, crops), F32),
-            sems(14), sems(14), pltpu.SemaphoreType.DMA((9, 8)), sems(3),
+            sems(14), sems(14), pltpu.SemaphoreType.DMA((9, 8)), sems(9),
         ],
         compiler_params=pltpu.CompilerParams(
             collective_id=1, has_side_effects=True, vmem_limit_bytes=60 * 1024 * 1024
@@ -515,16 +545,17 @@
         cost_estimate=pl.CostEstimate(flops=14_000_000_000, bytes_accessed=24_000_000, transcendentals=4_000_000),
         name="decoder_window",
     )(
-        features.reshape(cells, width), target.reshape(cells, outputs), gn_gain[None, :],
-        attn_query, attn_key, attn_value, attn_out, conv_bias[None, :], percept, lpips_weight[None, :],
-        crop_owner.reshape(1, -1), crop_frame, crop_col, conv_weight.reshape(taps, width, outputs),
+        features.reshape(cells, width), target.reshape(cells, outputs), attn_query, attn_key, attn_value, attn_out,
+        percept, conv_weight.reshape(taps, width, outputs), gn_gain[None, :], conv_bias[None, :], lpips_weight[None, :],
+        crop_owner.reshape(1, -1), crop_frame, crop_col,
     )
     conv_total = pl.pallas_call(
         widen,
-        grid=(taps // 3,),
-        in_specs=[pl.BlockSpec((2, 3, half, outputs), lambda i: (0, i, 0, 0))],
-        out_specs=pl.BlockSpec((3, width, outputs), lambda i: (i, 0, 0)),
+        in_specs=[hbm],
+        out_specs=hbm,
         out_shape=jax.ShapeDtypeStruct((taps, width, outputs), F32),
+        scratch_shapes=[pltpu.VMEM((2, taps, half, outputs), BF16), pltpu.VMEM((taps, width, outputs), F32), sems(9), sems(9)],
+        compiler_params=pltpu.CompilerParams(vmem_limit_bytes=60 * 1024 * 1024),
         name="widen",
     )(summed.reshape(2, taps, half, outputs)).reshape(conv_weight.shape)
     return (decoded.reshape(1, frames, rows_dev, cols, outputs), conv_total, distances)

time: 101 us -> 95.8 us (0.949)
  Pallas kernels: 98.4 us -> 93.8 us
    pallas_call x1, Pallas kernels: 10 us -> 6.93 us  [on_device(): pl.pallas_call(widen, in_specs=[hbm], out_specs=hbm, out_shape=jax.ShapeD...]
    pallas_call x1, Pallas kernels: 88.3 us -> 86.9 us  [on_device(): pl.pallas_call(functools.partial(decoder_window, tiles, frames, cols), in...]
where the time goes in v4:
time: 95.8 us; the launch traced here: 95.7 us
  Pallas kernels  93.8 us (98%)
  local copies, waits for them, and re-layouts  1.2 us (1%)
    pallas_call x1, Pallas kernels, on_device(): pl.pallas_call(functools.partial(decoder_window, tiles, frames, cols), in...  86.9 us
    pallas_call x1, Pallas kernels, on_device(): pl.pallas_call(widen, in_specs=[hbm], out_specs=hbm, out_shape=jax.ShapeD...  6.93 us

profile of v4, /device:TPU:1, one launch (start us, length us, event | category | flops | bytes accessed | tf_op | source)
XLA Modules:
  0.0 95.7 jit_solution(7902557195623246669)
XLA Ops:
  0.6 86.9 %decoder_window.1 = (bf16[384,256]{1,0:T(8,128)(2,1)}, bf16[2,3,2304,256]{3,2,1,0:T(8,128)(2,1)}, f32[1,8]{1,0:T(1,128)}) custom-call(bf16[384,512]{1,0:T(8,128)(2,1)} %bitcast.16, bf16[384,256]{1,0:T(8,128)(2,1)} %bitcast.17, bf16[512,512]{1,0:T(8,128)(2,1)} %wq_hbm.1, bf16[512,512]{1,0:T(8,128)(2,1)} %wk_hbm.1, bf16[512,512]{1,0:T(8,128)(2,1)} %wv_hbm.1, ...), custom_call_target="tpu_custom_call" | custom-call | flops 14000000000 | bytes 24000000 | tf_op jit(solution)/shard_map/decoder_window/pallas_call | solution.py:499
  87.5 0.0 copy-start
  87.5 0.0 copy-start.1
  87.5 6.9 %widen.1 = f32[27,512,256]{2,1,0:T(8,128)} custom-call(bf16[2,27,256,256]{3,2,1,0:T(8,128)(2,1)} %bitcast.13), custom_call_target="tpu_custom_call" | custom-call | tf_op jit(solution)/shard_map/widen/pallas_call | solution.py:552
  94.5 0.0 copy-done
  94.5 0.7 copy.20
  95.2 0.0 copy-done.1
  95.2 0.5 copy.21
Async XLA Ops:
  87.5 7.0 %copy-start = (bf16[384,256]{1,0:T(8,128)(2,1)S(1)}, bf16[384,256]{1,0:T(8,128)(2,1)}, u32[]{:S(2)}) copy-start(bf16[384,256]{1,0:T(8,128)(2,1)} %get-tuple-element.6) | copy-start | bytes 589828
  87.5 7.6 %copy-start.1 = (f32[1,8]{1,0:T(1,128)S(1)}, f32[1,8]{1,0:T(1,128)}, u32[]{:S(2)}) copy-start(f32[1,8]{1,0:T(1,128)} %get-tuple-element.17) | copy-start | bytes 100

commit v5 on v4

--- a/solution.py
+++ b/solution.py
@@ -66,9 +66,10 @@
 def decoder_window(
     tiles, frames, cols,
     features, target_hbm, wq_hbm, wk_hbm, wv_hbm, wo_hbm, percept_hbm, weight_hbm,
-    gain_ref, bias_ref, lpips_ref, owner_ref, frame_ref, col_ref,
+    gain_hbm, bias_hbm, lpips_hbm, owner_hbm, frame_hbm, col_hbm,
     decoded_ref, out_ref, dist_out,
-    weight, wq_ref, wk_ref, wv_ref, wo_ref, percept_ref, target_ref, feats, normed, stats, qs, acc, peak, total, hidden, hidden_t, other_h, own_g, other_g, rhs,
+    weight, wq_ref, wk_ref, wv_ref, wo_ref, percept_ref, target_ref,
+    gain_ref, bias_ref, lpips_ref, owner_ref, frame_ref, col_ref, feats, normed, stats, qs, acc, peak, total, hidden, hidden_t, other_h, own_g, other_g, rhs,
     part, left1, right1, comb, got, red1, got2, got3, quarter, dist_row, dist_pair,
     once, gather_recv, recv, local,
 ):
@@ -115,7 +116,11 @@
     early = [
         pltpu.make_async_copy(source, ref, local.at[3 + i])
         for i, (source, ref) in enumerate(
-            ((wq_hbm, wq_ref), (wk_hbm, wk_ref), (wv_hbm, wv_ref), (wo_hbm, wo_ref), (percept_hbm, percept_ref), (target_hbm, target_ref))
+            (
+                (wq_hbm, wq_ref), (wk_hbm, wk_ref), (wv_hbm, wv_ref), (wo_hbm, wo_ref), (percept_hbm, percept_ref),
+                (target_hbm, target_ref), (gain_hbm, gain_ref), (bias_hbm, bias_ref), (lpips_hbm, lpips_ref),
+                (owner_hbm, owner_ref), (frame_hbm, frame_ref), (col_hbm, col_ref),
+            )
         )
     ]
     for copy in early:
@@ -168,6 +173,8 @@
     mean = grouped[0:1] / count
     spread = grouped[1:2] / count - mean * mean
     scale = lax.rsqrt(spread + EPSILON)
+    for copy in early:
+        copy.wait()
     gain = gain_ref[...]
     factor = math.log2(math.e) / math.sqrt(width)
 
@@ -198,8 +205,6 @@
                 acc[here, j : j + 128] = acc[here, j : j + 128] * fade + out[:, j : j + 128]
         peak[here, :] = new
 
-    for copy in early:
-        copy.wait()
     normalize(0, own)
     make_queries(0, 0)
     links["z1"].wait_recv()
@@ -233,16 +238,8 @@
     normalize(7, opposite2)
     attend((0, 3), (7, 8), False)
 
-    def choose(i, values):
-        chosen = values[0]
-        for j in range(1, len(values)):
-            chosen = jnp.where(i == j, values[j], chosen)
-        return chosen
-
-    def finish(role, _):
-        here = pl.ds(pl.multiple_of(role * cells, cells), cells)
-        unit = choose(role, [own, partner, far])
-        b = choose(role, [1, 2 - 2 * side, 2 * side])
+    for role, unit, b in ((0, own, 1), (1, partner, 2 - 2 * side), (2, far, 2 * side)):
+        here = slice(role * cells, (role + 1) * cells)
         whole = 1.0 / jnp.sum(total[here, :], axis=1, keepdims=True)
         context = (acc[here, :] * whole).astype(BF16)
         mixed = dot(context, wv_ref[...]).astype(BF16)
@@ -251,9 +248,7 @@
         row = jnp.where(inside, row, 0.0).astype(BF16)
         hidden[b] = row
         hidden_t[b] = row.T
-        return 0
-
-    lax.fori_loop(0, 3, finish, 0)
+
     swap_h = remote(
         hidden_t.at[:, pl.ds(pl.multiple_of((1 - core) * half, half), half)], other_h, once.at[3], once.at[4], sibling
     )
@@ -461,7 +456,8 @@
     swap_h.wait_send()
 
 
-def widen(halves, out_hbm, near, wide, in_sems, out_sems):
+def widen(halves, made, scored, out_hbm, made_out, scored_out, near, wide, in_sems, out_sems, made_sem):
+    hand_on = pltpu.make_async_copy(made, made_out, made_sem)
     taps, half = halves.shape[1:3]
     steps = in_sems.shape[0]
     count = taps // steps
@@ -470,6 +466,8 @@
     stores = [pltpu.make_async_copy(wide.at[rows], out_hbm.at[rows], out_sems.at[i]) for i, rows in enumerate(pieces)]
     for copy in loads:
         copy.start()
+    hand_on.start()
+    scored_out[...] = scored[...]
     for i in range(steps):
         loads[i].wait()
         for tap in range(i * count, (i + 1) * count):
@@ -478,6 +476,7 @@
         stores[i].start()
     for copy in stores:
         copy.wait()
+    hand_on.wait()
 
 
 def on_device(
@@ -498,7 +497,7 @@
     sems = lambda count: pltpu.SemaphoreType.DMA((count,))
     decoded, summed, distances = pl.pallas_call(
         functools.partial(decoder_window, tiles, frames, cols),
-        in_specs=[hbm] * 8 + [vmem] * 6,
+        in_specs=[hbm] * 14,
         out_specs=[vmem, hbm, vmem],
         out_shape=[
             jax.ShapeDtypeStruct((cells, outputs), BF16),
@@ -513,6 +512,12 @@
             pltpu.VMEM((width, width), BF16),
             pltpu.VMEM((outputs, outputs), BF16),
             pltpu.VMEM((cells, outputs), BF16),
+            pltpu.VMEM((1, width), F32),
+            pltpu.VMEM((1, outputs), F32),
+            pltpu.VMEM((1, outputs), F32),
+            pltpu.VMEM((1, crops), jnp.int32),
+            pltpu.VMEM((1, crops), jnp.int32),
+            pltpu.VMEM((1, crops), jnp.int32),
             pltpu.VMEM((tiles, cells, width), BF16),
             pltpu.VMEM((tiles * cells, width), BF16),
             pltpu.VMEM((tiles, 8, width), F32),
@@ -537,7 +542,7 @@
             pltpu.VMEM((9, quarter, outputs), BF16),
             pltpu.VMEM((4, 8, crops), F32),
             pltpu.VMEM((2, 8, crops), F32),
-            sems(14), sems(14), pltpu.SemaphoreType.DMA((9, 8)), sems(9),
+            sems(14), sems(14), pltpu.SemaphoreType.DMA((9, 8)), sems(15),
         ],
         compiler_params=pltpu.CompilerParams(
             collective_id=1, has_side_effects=True, vmem_limit_bytes=60 * 1024 * 1024
@@ -549,15 +554,20 @@
         percept, conv_weight.reshape(taps, width, outputs), gn_gain[None, :], conv_bias[None, :], lpips_weight[None, :],
         crop_owner.reshape(1, -1), crop_frame, crop_col,
     )
-    conv_total = pl.pallas_call(
+    conv_total, decoded, distances = pl.pallas_call(
         widen,
-        in_specs=[hbm],
-        out_specs=hbm,
-        out_shape=jax.ShapeDtypeStruct((taps, width, outputs), F32),
-        scratch_shapes=[pltpu.VMEM((2, taps, half, outputs), BF16), pltpu.VMEM((taps, width, outputs), F32), sems(9), sems(9)],
+        in_specs=[hbm, hbm, vmem],
+        out_specs=[hbm, hbm, vmem],
+        out_shape=[
+            jax.ShapeDtypeStruct((taps, width, outputs), F32),
+            jax.ShapeDtypeStruct(decoded.shape, BF16),
+            jax.ShapeDtypeStruct(distances.shape, F32),
+        ],
+        scratch_shapes=[pltpu.VMEM((2, taps, half, outputs), BF16), pltpu.VMEM((taps, width, outputs), F32), sems(9), sems(9), pltpu.SemaphoreType.DMA],
         compiler_params=pltpu.CompilerParams(vmem_limit_bytes=60 * 1024 * 1024),
         name="widen",
-    )(summed.reshape(2, taps, half, outputs)).reshape(conv_weight.shape)
+    )(summed.reshape(2, taps, half, outputs), decoded, distances)
+    conv_total = conv_total.reshape(conv_weight.shape)
     return (decoded.reshape(1, frames, rows_dev, cols, outputs), conv_total, distances)
 
 

time: 95.8 us -> 94.7 us (0.989)
  local copies, waits for them, and re-layouts: 1.2 us -> 0 us
    pallas_call x1, Pallas kernels: 6.93 us -> 8.35 us  [on_device(): pl.pallas_call(widen, in_specs=[hbm, hbm, vmem], out_specs=[hbm, hbm, vme...]
    pallas_call x1, Pallas kernels: 86.9 us -> 85.5 us  [on_device(): pl.pallas_call(functools.partial(decoder_window, tiles, frames, cols), in...]
    unnamed x6 -> x0, local copies, waits for them, and re-layouts: 1.2 us -> none
where the time goes in v5:
time: 94.7 us; the launch traced here: 94.6 us
  Pallas kernels  93.8 us (99%)
    pallas_call x1, Pallas kernels, on_device(): pl.pallas_call(functools.partial(decoder_window, tiles, frames, cols), in...  85.5 us
    pallas_call x1, Pallas kernels, on_device(): pl.pallas_call(widen, in_specs=[hbm, hbm, vmem], out_specs=[hbm, hbm, vme...  8.35 us

profile of v5, /device:TPU:1, one launch (start us, length us, event | category | flops | bytes accessed | tf_op | source)
XLA Modules:
  0.0 94.6 jit_solution(9691399858692508789)
XLA Ops:
  0.6 85.5 %decoder_window.1 = (bf16[384,256]{1,0:T(8,128)(2,1)}, bf16[2,3,2304,256]{3,2,1,0:T(8,128)(2,1)}, f32[1,8]{1,0:T(1,128)}) custom-call(bf16[384,512]{1,0:T(8,128)(2,1)} %bitcast.15, bf16[384,256]{1,0:T(8,128)(2,1)} %bitcast.16, bf16[512,512]{1,0:T(8,128)(2,1)} %wq_hbm.1, bf16[512,512]{1,0:T(8,128)(2,1)} %wk_hbm.1, bf16[512,512]{1,0:T(8,128)(2,1)} %wv_hbm.1, ...), custom_call_target="tpu_custom_call" | custom-call | flops 14000000000 | bytes 24000000 | tf_op jit(solution)/shard_map/decoder_window/pallas_call | solution.py:498
  86.1 8.3 %widen.1 = (f32[27,512,256]{2,1,0:T(8,128)}, bf16[384,256]{1,0:T(8,128)(2,1)}, f32[1,8]{1,0:T(1,128)}) custom-call(bf16[2,27,256,256]{3,2,1,0:T(8,128)(2,1)} %bitcast.12, bf16[384,256]{1,0:T(8,128)(2,1)} %get-tuple-element.10.made, f32[1,8]{1,0:T(1,128)} %get-tuple-element.11.scored), custom_call_target="tpu_custom_call" | custom-call | tf_op jit(solution)/shard_map/widen/pallas_call | solution.py:557

commit v6 on v5

--- a/solution.py
+++ b/solution.py
@@ -456,27 +456,27 @@
     swap_h.wait_send()
 
 
-def widen(halves, made, scored, out_hbm, made_out, scored_out, near, wide, in_sems, out_sems, made_sem):
-    hand_on = pltpu.make_async_copy(made, made_out, made_sem)
+def widen(halves, made, scored, out_hbm, made_out, scored_out, near, wide, in_sems, out_sems, hand_sems):
+    hand_on = [
+        pltpu.make_async_copy(made, made_out, hand_sems.at[0]),
+        pltpu.make_async_copy(scored, scored_out, hand_sems.at[1]),
+    ]
     taps, half = halves.shape[1:3]
     steps = in_sems.shape[0]
     count = taps // steps
     pieces = [pl.ds(i * count, count) for i in range(steps)]
     loads = [pltpu.make_async_copy(halves.at[:, rows], near.at[:, rows], in_sems.at[i]) for i, rows in enumerate(pieces)]
     stores = [pltpu.make_async_copy(wide.at[rows], out_hbm.at[rows], out_sems.at[i]) for i, rows in enumerate(pieces)]
-    for copy in loads:
+    for copy in loads + hand_on:
         copy.start()
-    hand_on.start()
-    scored_out[...] = scored[...]
     for i in range(steps):
         loads[i].wait()
         for tap in range(i * count, (i + 1) * count):
             for h in range(2):
                 wide[tap, h * half : (h + 1) * half, :] = near[h, tap].astype(F32)
         stores[i].start()
-    for copy in stores:
+    for copy in stores + hand_on:
         copy.wait()
-    hand_on.wait()
 
 
 def on_device(
@@ -556,14 +556,14 @@
     )
     conv_total, decoded, distances = pl.pallas_call(
         widen,
-        in_specs=[hbm, hbm, vmem],
-        out_specs=[hbm, hbm, vmem],
+        in_specs=[hbm] * 3,
+        out_specs=[hbm] * 3,
         out_shape=[
             jax.ShapeDtypeStruct((taps, width, outputs), F32),
             jax.ShapeDtypeStruct(decoded.shape, BF16),
             jax.ShapeDtypeStruct(distances.shape, F32),
         ],
-        scratch_shapes=[pltpu.VMEM((2, taps, half, outputs), BF16), pltpu.VMEM((taps, width, outputs), F32), sems(9), sems(9), pltpu.SemaphoreType.DMA],
+        scratch_shapes=[pltpu.VMEM((2, taps, half, outputs), BF16), pltpu.VMEM((taps, width, outputs), F32), sems(9), sems(9), sems(2)],
         compiler_params=pltpu.CompilerParams(vmem_limit_bytes=60 * 1024 * 1024),
         name="widen",
     )(summed.reshape(2, taps, half, outputs), decoded, distances)

time: 94.7 us -> 93.6 us (0.988)
  Pallas kernels: 93.8 us -> 92.7 us
    pallas_call x1, Pallas kernels: 8.35 us -> 7.26 us  [on_device(): pl.pallas_call(widen, in_specs=[hbm] * 3, out_specs=[hbm] * 3, out_shape=...]
where the time goes in v6:
time: 93.6 us; the launch traced here: 93.5 us
  Pallas kernels  92.7 us (99%)
    pallas_call x1, Pallas kernels, on_device(): pl.pallas_call(functools.partial(decoder_window, tiles, frames, cols), in...  85.5 us
    pallas_call x1, Pallas kernels, on_device(): pl.pallas_call(widen, in_specs=[hbm] * 3, out_specs=[hbm] * 3, out_shape=...  7.26 us

profile of v6, /device:TPU:1, one launch (start us, length us, event | category | flops | bytes accessed | tf_op | source)
XLA Modules:
  0.0 93.5 jit_solution(18435690071986900685)
XLA Ops:
  0.6 85.5 %decoder_window.1 = (bf16[384,256]{1,0:T(8,128)(2,1)}, bf16[2,3,2304,256]{3,2,1,0:T(8,128)(2,1)}, f32[1,8]{1,0:T(1,128)}) custom-call(bf16[384,512]{1,0:T(8,128)(2,1)} %bitcast.15, bf16[384,256]{1,0:T(8,128)(2,1)} %bitcast.16, bf16[512,512]{1,0:T(8,128)(2,1)} %wq_hbm.1, bf16[512,512]{1,0:T(8,128)(2,1)} %wk_hbm.1, bf16[512,512]{1,0:T(8,128)(2,1)} %wv_hbm.1, ...), custom_call_target="tpu_custom_call" | custom-call | flops 14000000000 | bytes 24000000 | tf_op jit(solution)/shard_map/decoder_window/pallas_call | solution.py:498
  86.1 7.3 %widen.1 = (f32[27,512,256]{2,1,0:T(8,128)}, bf16[384,256]{1,0:T(8,128)(2,1)}, f32[1,8]{1,0:T(1,128)}) custom-call(bf16[2,27,256,256]{3,2,1,0:T(8,128)(2,1)} %bitcast.12, bf16[384,256]{1,0:T(8,128)(2,1)} %get-tuple-element.10.made, f32[1,8]{1,0:T(1,128)} %get-tuple-element.11.scored), custom_call_target="tpu_custom_call" | custom-call | tf_op jit(solution)/shard_map/widen/pallas_call | solution.py:557

commit v7 on v6

--- a/solution.py
+++ b/solution.py
@@ -125,7 +125,10 @@
     ]
     for copy in early:
         copy.start()
-    fetch = pltpu.make_async_copy(weight_hbm, weight, local.at[1])
+    fetches = [
+        pltpu.make_async_copy(weight_hbm.at[:, e], weight.at[:, :, pl.ds(e * outputs, outputs)], local.at[(1, 15, 16)[e]])
+        for e in range(3)
+    ]
 
     def pass_on(index, unit, h, to, mine_too=False):
         rows = feats.at[unit, pl.ds(h * cut, cut)]
@@ -149,7 +152,8 @@
     links["l1"] = pass_on(4, own, 1, right, True)
     links["r0"] = pass_on(5, own, 0, left, True)
     links["z1"] = pass_on(3, own, 1, partner, True)
-    fetch.start()
+    for copy in fetches:
+        copy.start()
 
     lane = lax.broadcasted_iota(jnp.int32, (width, width), 0) // (width // GROUPS)
     same = (lane == lax.broadcasted_iota(jnp.int32, (width, width), 1) // (width // GROUPS)).astype(BF16)
@@ -224,6 +228,15 @@
     attend((1, 2), (0, 4), True)
     normalize(4, opposite)
     attend((0, 2), (4, 5), False)
+    table = percept_ref[...]
+    zt = dot(target_ref[...], table)
+    mt, _ = gelu_parts(zt)
+    st = lax.rsqrt(jnp.mean(mt * mt, axis=-1, keepdims=True) + EPSILON)
+    seen = mt * st
+    spot = lax.broadcasted_iota(jnp.int32, (cols, 1), 0)
+    col = col_ref[...]
+    inside = (spot >= col) & (spot < col + CROPW) & (owner_ref[...] == mine)
+    covers = [(inside & (frame_ref[...] == f)).astype(F32) for f in range(frames)]
     links["l2"].wait_recv()
     links["r3"].wait_recv()
     links["l3"].wait_recv()
@@ -252,30 +265,23 @@
     swap_h = remote(
         hidden_t.at[:, pl.ds(pl.multiple_of((1 - core) * half, half), half)], other_h, once.at[3], once.at[4], sibling
     )
-    fetch.wait()
-
-    sides = []
-    for e in range(3):
-        a2, a1, a0 = (
-            sum(
-                dot(hidden[b, : (a + 1) * cols, :], weight[(a * 3 + b) * 3 + e]) for b in range(3)
-            )
-            for a in (2, 1, 0)
-        )
-        sides.append(a2 + jnp.concatenate([a1[:cols], a1], axis=0) + jnp.concatenate([a0, a0, a0], axis=0))
+    for copy in fetches:
+        copy.wait()
+
+    a2, a1, a0 = (
+        sum(dot(hidden[b, : (a + 1) * cols, :], weight[a * 3 + b]) for b in range(3)) for a in (2, 1, 0)
+    )
+    wide_sum = a2 + jnp.concatenate([a1[:cols], a1], axis=0) + jnp.concatenate([a0, a0, a0], axis=0)
+    sides = [wide_sum[:, e * outputs : (e + 1) * outputs] for e in range(3)]
     made = shift_rows(sides[0], 1, cols) + sides[1] + shift_rows(sides[2], -1, cols) + bias_ref[...]
     made = made.astype(BF16)
     decoded_ref[...] = made
 
-    table = percept_ref[...]
     lw = lpips_ref[...]
     z = dot(made, table)
     m, t = gelu_parts(z)
     s = lax.rsqrt(jnp.mean(m * m, axis=-1, keepdims=True) + EPSILON)
-    zt = dot(target_ref[...], table)
-    mt, _ = gelu_parts(zt)
-    st = lax.rsqrt(jnp.mean(mt * mt, axis=-1, keepdims=True) + EPSILON)
-    gap = m * s - mt * st
+    gap = m * s - seen
     weighted = gap * lw
     apart = jnp.sum(weighted * gap, axis=-1, keepdims=True)
     up = weighted * (2.0 / CROPW)
@@ -285,12 +291,9 @@
     low = (dz - high.astype(F32)).astype(BF16)
     pull = (dot_nt(high, table) + dot_nt(low, table)).astype(BF16).astype(F32)
 
-    spot = lax.broadcasted_iota(jnp.int32, (cols, 1), 0)
-    col = col_ref[...]
-    covers = (spot >= col) & (spot < col + CROPW) & (owner_ref[...] == mine)
     distance = jnp.zeros((1, col.shape[1]), F32)
     for f in range(frames):
-        cover = (covers & (frame_ref[...] == f)).astype(F32)
+        cover = covers[f]
         rows = slice(f * cols, (f + 1) * cols)
         distance = distance + jnp.sum(cover * apart[rows], axis=0, keepdims=True)
         own_g[rows, :] = (pull[rows] * jnp.sum(cover, axis=1, keepdims=True)).astype(BF16)
@@ -340,11 +343,10 @@
         for p in range(3):
             c, m, depth = p * 3 + b, place[p], (p + 1) * cols
             lhs = jnp.concatenate([hidden_t[b, own_half, :depth], other_h[b, :, :depth]], axis=1)
+            made_wide = dot(lhs, rhs[p, : 2 * depth, :])
             for e in range(3):
                 base = b * chunk_rows + e * half
-                part[p, base : base + half, :] = dot(
-                    lhs, rhs[p, : 2 * depth, e * outputs : (e + 1) * outputs]
-                ).astype(BF16)
+                part[p, base : base + half, :] = made_wide[:, e * outputs : (e + 1) * outputs].astype(BF16)
             go(c, 0, part.at[p, chunk_at(b, m + 2, 0)], left1.at[c], peer(p, 1))
             go(c, 0, part.at[p, chunk_at(b, m + 2, 1)], right1.at[c], peer(p, 3))
             go(c, 1, part.at[p, chunk_at(b, m + 1, 1)], got.at[c, 0, pl.ds(half_rows, half_rows)], peer(p, 1))
@@ -505,7 +507,7 @@
             jax.ShapeDtypeStruct((1, crops // tiles), F32),
         ],
         scratch_shapes=[
-            pltpu.VMEM((taps, width, outputs), BF16),
+            pltpu.VMEM((9, width, 3 * outputs), BF16),
             pltpu.VMEM((width, width), BF16),
             pltpu.VMEM((width, width), BF16),
             pltpu.VMEM((width, width), BF16),
@@ -542,7 +544,7 @@
             pltpu.VMEM((9, quarter, outputs), BF16),
             pltpu.VMEM((4, 8, crops), F32),
             pltpu.VMEM((2, 8, crops), F32),
-            sems(14), sems(14), pltpu.SemaphoreType.DMA((9, 8)), sems(15),
+            sems(14), sems(14), pltpu.SemaphoreType.DMA((9, 8)), sems(17),
         ],
         compiler_params=pltpu.CompilerParams(
             collective_id=1, has_side_effects=True, vmem_limit_bytes=60 * 1024 * 1024
@@ -551,7 +553,7 @@
         name="decoder_window",
     )(
         features.reshape(cells, width), target.reshape(cells, outputs), attn_query, attn_key, attn_value, attn_out,
-        percept, conv_weight.reshape(taps, width, outputs), gn_gain[None, :], conv_bias[None, :], lpips_weight[None, :],
+        percept, conv_weight.reshape(9, 3, width, outputs), gn_gain[None, :], conv_bias[None, :], lpips_weight[None, :],
         crop_owner.reshape(1, -1), crop_frame, crop_col,
     )
     conv_total, decoded, distances = pl.pallas_call(

time: 93.6 us -> 93.2 us (level)
  no operation moved by 1% of the time
where the time goes in v7:
time: 93.2 us; the launch traced here: 93.1 us
  Pallas kernels  92.3 us (99%)
    pallas_call x1, Pallas kernels, on_device(): pl.pallas_call(functools.partial(decoder_window, tiles, frames, cols), in...  85 us
    pallas_call x1, Pallas kernels, on_device(): pl.pallas_call(widen, in_specs=[hbm] * 3, out_specs=[hbm] * 3, out_shape=...  7.26 us

profile of v7, /device:TPU:1, one launch (start us, length us, event | category | flops | bytes accessed | tf_op | source)
XLA Modules:
  0.0 93.1 jit_solution(9823607256158220313)
XLA Ops:
  0.6 85.0 %decoder_window.1 = (bf16[384,256]{1,0:T(8,128)(2,1)}, bf16[2,3,2304,256]{3,2,1,0:T(8,128)(2,1)}, f32[1,8]{1,0:T(1,128)}) custom-call(bf16[384,512]{1,0:T(8,128)(2,1)} %bitcast.15, bf16[384,256]{1,0:T(8,128)(2,1)} %bitcast.16, bf16[512,512]{1,0:T(8,128)(2,1)} %wq_hbm.1, bf16[512,512]{1,0:T(8,128)(2,1)} %wk_hbm.1, bf16[512,512]{1,0:T(8,128)(2,1)} %wv_hbm.1, ...), custom_call_target="tpu_custom_call" | custom-call | flops 14000000000 | bytes 24000000 | tf_op jit(solution)/shard_map/decoder_window/pallas_call | solution.py:500
  85.7 7.3 %widen.1 = (f32[27,512,256]{2,1,0:T(8,128)}, bf16[384,256]{1,0:T(8,128)(2,1)}, f32[1,8]{1,0:T(1,128)}) custom-call(bf16[2,27,256,256]{3,2,1,0:T(8,128)(2,1)} %bitcast.12, bf16[384,256]{1,0:T(8,128)(2,1)} %get-tuple-element.10.made, f32[1,8]{1,0:T(1,128)} %get-tuple-element.11.scored), custom_call_target="tpu_custom_call" | custom-call | tf_op jit(solution)/shard_map/widen/pallas_call | solution.py:559

commit v8 on v7

--- a/solution.py
+++ b/solution.py
@@ -366,7 +366,7 @@
             take(got.at[c], recv.at[c, 1])
             mine_rows = part[p, chunk_at(b, place[p], 0, 2), :].astype(F32)
             red1[c] = (mine_rows + got[c, 0].astype(F32) + got[c, 1].astype(F32)).astype(BF16)
-            for step in (1, 2, 3):
+            for step in (2, 1, 3):
                 to = lax.rem(place[axis] + step, 4)
                 go(c, 2, red1.at[c, pl.ds(pl.multiple_of(to * piece, 16), piece)], got2.at[c, step - 1], peer(axis, step))
 
@@ -378,7 +378,7 @@
             for i in range(3):
                 added = added + got2[c, i].astype(F32)
             got3[c, place[axis]] = added.astype(BF16)
-            for step in (1, 2, 3):
+            for step in (2, 1, 3):
                 slot = got3.at[c, place[axis]]
                 go(c, 3, slot, slot, peer(axis, step))
 
@@ -391,7 +391,7 @@
                 whole = whole + got3[c, i].astype(F32)
             rows = pl.ds(pl.multiple_of(place[axis] * piece, 16), piece)
             quarter[c, rows, :] = whole.astype(BF16)
-            for step in (1, 2, 3):
+            for step in (2, 1, 3):
                 slot = quarter.at[c, rows]
                 go(c, 4, slot, slot, peer(axis, step))
 
@@ -399,8 +399,14 @@
         for p in range(3):
             c, m = p * 3 + b, place[p]
             take(got2.at[c], recv.at[c, 4])
-            for stage, h, step in ((5, 0, 1), (5, 1, 3), (6, 1, 1), (6, 0, 3)):
-                go(c, stage, quarter.at[c, pl.ds(h * half_rows, half_rows)], out_rows(p, b, m, h), peer(p, step))
+            for h, step in ((0, 1), (1, 3)):
+                go(c, 5, quarter.at[c, pl.ds(h * half_rows, half_rows)], out_rows(p, b, m, h), peer(p, step))
+        for p in range(3):
+            c, m = p * 3 + b, place[p]
+            for h, step in ((1, 1), (0, 3)):
+                go(c, 6, quarter.at[c, pl.ds(h * half_rows, half_rows)], out_rows(p, b, m, h), peer(p, step))
+        for p in range(3):
+            c, m = p * 3 + b, place[p]
             across_to(quarter.at[c], out_rows(p, b, m, 0, 2))
             pltpu.make_async_copy(quarter.at[c], out_rows(p, b, m, 0, 2), local.at[2]).start()
 

time: 93.2 us -> 92.9 us (level)
  no operation moved by 1% of the time
where the time goes in v8:
time: 92.9 us; the launch traced here: 92.7 us
  Pallas kernels  91.9 us (99%)
    pallas_call x1, Pallas kernels, on_device(): pl.pallas_call(functools.partial(decoder_window, tiles, frames, cols), in...  84.7 us
    pallas_call x1, Pallas kernels, on_device(): pl.pallas_call(widen, in_specs=[hbm] * 3, out_specs=[hbm] * 3, out_shape=...  7.26 us

profile of v8, /device:TPU:1, one launch (start us, length us, event | category | flops | bytes accessed | tf_op | source)
XLA Modules:
  0.0 92.7 jit_solution(1723978379065316576)
XLA Ops:
  0.6 84.7 %decoder_window.1 = (bf16[384,256]{1,0:T(8,128)(2,1)}, bf16[2,3,2304,256]{3,2,1,0:T(8,128)(2,1)}, f32[1,8]{1,0:T(1,128)}) custom-call(bf16[384,512]{1,0:T(8,128)(2,1)} %bitcast.15, bf16[384,256]{1,0:T(8,128)(2,1)} %bitcast.16, bf16[512,512]{1,0:T(8,128)(2,1)} %wq_hbm.1, bf16[512,512]{1,0:T(8,128)(2,1)} %wk_hbm.1, bf16[512,512]{1,0:T(8,128)(2,1)} %wv_hbm.1, ...), custom_call_target="tpu_custom_call" | custom-call | flops 14000000000 | bytes 24000000 | tf_op jit(solution)/shard_map/decoder_window/pallas_call | solution.py:506
  85.3 7.3 %widen.1 = (f32[27,512,256]{2,1,0:T(8,128)}, bf16[384,256]{1,0:T(8,128)(2,1)}, f32[1,8]{1,0:T(1,128)}) custom-call(bf16[2,27,256,256]{3,2,1,0:T(8,128)(2,1)} %bitcast.12, bf16[384,256]{1,0:T(8,128)(2,1)} %get-tuple-element.10.made, f32[1,8]{1,0:T(1,128)} %get-tuple-element.11.scored), custom_call_target="tpu_custom_call" | custom-call | tf_op jit(solution)/shard_map/widen/pallas_call | solution.py:565
